TPU v7x, 32 devices: a whole 2x2x4 slice. The times are simulated.
32 devices in a mesh: slab: 4 (over x, core), dom: 8 (over z, y).
Axes of the slice: x: 2, y: 2, z: 4, core: 2. Of those that a mesh axis runs over, the one named last changes fastest.
Arguments:
- coords: float32 [3, 4, 8, 512], P(None, 'slab', 'dom'), may hold values from -6 to 6
- velocity: float32 [3, 4, 8, 512], P(None, 'slab', 'dom'), may hold values from -6 to 6
- charge: float32 [4, 8, 512], P('slab', 'dom'), may hold values from -1 to 1
- inv_mass: float32 [4, 8, 512], P('slab', 'dom'), may hold values from 0.0625 to 1
- tile_block: int32 [4, 8, 64], P('slab', 'dom'), may hold values from 0 to 3
- tile_atoms: int32 [4, 8, 64, 128], P('slab', 'dom'), may hold values from 0 to 2047
- active_tile_count: int32 [4, 8], P('slab', 'dom'), may hold values from 1 to 64
- bond_atoms: int32 [2, 4, 8, 256], P(None, 'slab', 'dom'), may hold values from 0 to 511, as said below
- cross_atoms: int32 [2, 4, 8, 128], P(None, 'slab', 'dom'), may hold values from 0 to 255
- cross_side: int32 [4, 8, 128], P('slab', 'dom'), may hold values from 0 to 3
- cross_count: int32 [4, 8], P('slab', 'dom'), may hold values from 1 to 128
Outputs:
- coords_out: float32 [3, 4, 8, 512], P(None, 'slab', 'dom')
- velocity_out: float32 [3, 4, 8, 512], P(None, 'slab', 'dom')
Inputs may be any that keep to these rules, and one draw needn't show every extreme that they name: `bond_atoms`: each bond joins two different atoms of the domain that holds it. `cross_atoms`: row 0 is an atom of the owning domain, row 1 an atom of the neighbour named by cross_side; both are among the first 256 atoms of their domains. `cross_side`: codes 0 to 3 name the in-slab neighbours at offsets +1, -1, +2, -2 along dom, cyclically. `cross_count`: slots below the count are live. `active_tile_count`: tiles below the count are live. `tile_atoms`: entries index the domain's halo list as in the first step.
All inputs are finite; a program needn't handle non-finite values.
Results may differ from a plain program's by a relative error of at most 0.0003.
Values sent between devices are 32-bit elements; how exact they have to be, the bound alone decides.
No kernel may reach another device: no remote copies, remote signals or barrier semaphores. Data moves between devices by JAX's collectives and lax.ppermute only.
A program may use at most 64 MiB of HBM per device.

v0:
```python
import functools

import jax
import jax.numpy as jnp
from jax import lax
from jax.experimental import pallas as pl
from jax.experimental.pallas import tpu as pltpu
from jax.sharding import PartitionSpec as P

TILE = 128
ORDER = 4
LANES = 128
SUBLANES = 8

time_step = 0.1
cutoff_sq = 16.0
force_scale = 4.0
length_floor = 0.25


def passed_along(array, axis, by):
    length = lax.axis_size(axis)
    return lax.ppermute(array, axis, [(i, (i + by) % length) for i in range(length)])


def first_of(domains):
    return domains - 1


def from_slab(blocks):
    length = lax.axis_size("dom")
    order = [(first_of(length) + i) % length for i in range(length)]
    return lax.all_to_all(blocks, "dom", 0, 0, axis_index_groups=[order], tiled=True)


def place_of(stride=0):
    length = lax.axis_size("dom")
    return lax.rem(lax.axis_index("dom") + (stride - first_of(length)) % length, length)


def strides_of(domains):
    row_width = max(2, domains // 8)
    return (1, -1, row_width, -row_width)


def round_up(count, step):
    return -(-count // step) * step


class Rows:
    def __init__(self, atoms, bonds, slots):
        self.atom_rows = atoms // LANES
        self.shell_rows = atoms // 2 // LANES
        self.bond_rows = bonds // LANES
        self.slot_rows = slots // LANES
        at = 0
        self.coords = []
        for _ in range(3):
            self.coords.append(at)
            at += self.atom_rows
        self.charge = at
        at += self.atom_rows
        self.mass = at
        at += self.atom_rows
        self.bond_first = at
        at += self.bond_rows
        self.bond_second = at
        at += self.bond_rows
        self.cross_first = at
        at += self.slot_rows
        self.cross_second = at
        at += self.slot_rows
        self.side = at
        at += self.slot_rows
        self.used = at
        self.count = round_up(at, SUBLANES)
        self.shell_terms = (self.bond_rows + self.slot_rows) * LANES
        self.inner_at = (0, self.shell_terms)
        self.cross_at = self.bond_rows * LANES
        self.far_at = self.shell_terms + self.bond_rows * LANES
        self.matrix = self.far_at + self.slot_rows * LANES
        self.live = 3 * self.atom_rows
        self.disp_used = self.live + self.slot_rows
        self.disp_count = round_up(self.disp_used, SUBLANES)


def take_lanes(table, lanes):
    return jnp.take_along_axis(table, lanes, axis=1, mode="promise_in_bounds")


def pick(tables, index):
    lanes = index & (LANES - 1)
    chunk = index >> 7
    result = take_lanes(tables[0], lanes)
    for k in range(1, len(tables)):
        result = jnp.where(chunk == k, take_lanes(tables[k], lanes), result)
    return result


def fetched(sources, targets, sem_ref):
    copies = [pltpu.make_async_copy(s, t, sem_ref.at[n]) for n, (s, t) in enumerate(zip(sources, targets))]
    for copy in copies:
        copy.start()
    return copies


def pack_kernel(rows, copies, *refs):
    sources, (out_ref, rim_ref), targets, sem_ref = refs[:6], refs[6:8], refs[8:14], refs[14]
    for copy in fetched(sources, targets, sem_ref):
        copy.wait()
    coords_ref, charge_ref, mass_ref, bonds_ref, cross_ref, side_ref = targets

    def put(row, value):
        for part in range(value.shape[1] // LANES):
            piece = value[:, part * LANES : (part + 1) * LANES]
            for copy in range(copies):
                out_ref[pl.ds(copy * rows.count + row + part, 1), :] = piece

    shell = rows.shell_rows * LANES
    fields = [coords_ref[c, 0] for c in range(3)] + [charge_ref[0]]
    for c in range(4):
        at = rows.coords[c] if c < 3 else rows.charge
        put(at, fields[c])
        for part in range(rows.shell_rows):
            rim_ref[pl.ds(c * rows.shell_rows + part, 1), :] = fields[c][:, part * LANES : (part + 1) * LANES]
    put(rows.mass, mass_ref[0])
    put(rows.bond_first, bonds_ref[0, 0].astype(jnp.float32))
    put(rows.bond_second, bonds_ref[1, 0].astype(jnp.float32))
    put(rows.cross_first, cross_ref[0, 0].astype(jnp.float32))
    put(rows.cross_second, cross_ref[1, 0].astype(jnp.float32))
    put(rows.side, side_ref[0].astype(jnp.float32))
    if rows.count > rows.used:
        for copy in range(copies):
            out_ref[pl.ds(copy * rows.count + rows.used, rows.count - rows.used), :] = jnp.zeros(
                (rows.count - rows.used, LANES), jnp.float32
            )


SHRINK = 1.0 / 4.0
OUT_OF_REACH = 1000.0
TILES_STEP = 4
PIECE = 32


def own_kernel(
    rows,
    coords_hbm,
    charge_hbm,
    velocity_hbm,
    mass_hbm,
    atoms_hbm,
    own_ref,
    far_ref,
    index_ref,
    motion_ref,
    coords_ref,
    charge_ref,
    velocity_ref,
    mass_ref,
    sem_ref,
):
    atom_rows = rows.atom_rows
    copies = fetched(
        (coords_hbm, charge_hbm, atoms_hbm.at[0, 0], velocity_hbm, mass_hbm),
        (coords_ref, charge_ref, index_ref, velocity_ref, mass_ref),
        sem_ref,
    )
    down = lax.broadcasted_iota(jnp.int32, (SUBLANES, LANES), 0)
    copies[0].wait()
    copies[1].wait()

    def lanes_of(part):
        return slice(part * LANES, (part + 1) * LANES)

    table = []
    for c in range(4):
        field = coords_ref[c, 0] * SHRINK if c < 3 else charge_ref[0]
        table.append(
            [jnp.broadcast_to(field[:, lanes_of(part)], (SUBLANES, LANES)) for part in range(atom_rows)]
        )
    for part in range(atom_rows):
        for group in range(LANES // SUBLANES):
            at = part * LANES + group * SUBLANES
            for c in range(4):
                value = take_lanes(table[c][part], down + group * SUBLANES)
                own_ref[c, pl.ds(at, SUBLANES), :] = value if c < 3 else value * 8.0
    copies[2].wait()
    for group in range(index_ref.shape[0] // SUBLANES):
        at = pl.ds(group * SUBLANES, SUBLANES)
        index = index_ref[at, :]
        for c in range(4):
            far_ref[c, at, :] = pick(table[c], index)
    copies[3].wait()
    copies[4].wait()
    fields = [velocity_ref[c, 0] for c in range(3)] + [mass_ref[0]]
    for c, field in enumerate(fields):
        for part in range(atom_rows):
            motion_ref[pl.ds(c * atom_rows + part, 1), :] = field[:, lanes_of(part)]


def force_kernel(
    rows,
    copies,
    place,
    live_ref,
    count_ref,
    block_hbm,
    around_ref,
    below_ref,
    above_ref,
    own_ref,
    near_ref,
    index_ref,
    motion_ref,
    out_ref,
    table_ref,
    far_ref,
    sum_ref,
    block_ref,
    sem_ref,
):
    atom_rows, shell_rows = rows.atom_rows, rows.shell_rows
    tiles = index_ref.shape[0]
    block_copy = pltpu.make_async_copy(block_hbm, block_ref, sem_ref)
    block_copy.start()
    holders = place()
    starts = [rows.coords[0], rows.coords[1], rows.coords[2], rows.charge]
    entry_rows = 6 * shell_rows

    def broadcast(row):
        return jnp.broadcast_to(row, (SUBLANES, LANES))

    for c in range(4):
        factor = SHRINK if c < 3 else 1.0
        at = 0
        for neighbour in range(4):
            base = holders[neighbour] * rows.count + starts[c]
            for part in range(shell_rows):
                table_ref[c, at] = broadcast(around_ref[pl.ds(base + part, 1), :] * factor)
                at += 1
        for slab_ref in (below_ref, above_ref):
            for part in range(shell_rows):
                table_ref[c, at] = broadcast(slab_ref[pl.ds(c * shell_rows + part, 1), :] * factor)
                at += 1

    live = live_ref[0, 0]
    down = lax.broadcasted_iota(jnp.int32, (SUBLANES, LANES), 0)
    for group in range(tiles // SUBLANES):
        at = pl.ds(group * SUBLANES, SUBLANES)
        index = index_ref[at, :]
        lanes = index & (LANES - 1)
        chunk = index >> 7
        values = [near_ref[c, at, :] for c in range(4)]
        for k in range(entry_rows):
            here = chunk == atom_rows + k
            values = [jnp.where(here, take_lanes(table_ref[c, k], lanes), values[c]) for c in range(4)]
        values[0] = jnp.where(down + group * SUBLANES < live, values[0], OUT_OF_REACH)
        for c in range(4):
            far_ref[c, at, :] = values[c]

    sum_ref[...] = jnp.zeros(sum_ref.shape, jnp.float32)
    block_copy.wait()

    softening = 1.0 / cutoff_sq

    def add_tile(tile):
        base = block_ref[0, 0, tile] * TILE
        far = [jnp.broadcast_to(far_ref[c, pl.ds(tile, 1), :], (PIECE, LANES)) for c in range(4)]
        for piece in range(TILE // PIECE):
            at = pl.ds(pl.multiple_of(base + piece * PIECE, PIECE), PIECE)
            gap = [own_ref[c, at, :] - far[c] for c in range(3)]
            square = gap[0] * gap[0] + gap[1] * gap[1] + gap[2] * gap[2]
            inverse = pl.reciprocal(square + softening, approx=True)
            weight = jnp.maximum(inverse - 1.0 / (1.0 + softening), 0.0)
            strength = (inverse - own_ref[3, at, :] * far[3]) * (weight * weight)
            for c in range(3):
                sum_ref[c, at, :] = sum_ref[c, at, :] + strength * gap[c]

    def add_tiles(step, _):
        for n in range(TILES_STEP):
            add_tile(step * TILES_STEP + n)
        return 0

    lax.fori_loop(0, lax.div(live + TILES_STEP - 1, TILES_STEP), add_tiles, 0)

    scale = time_step * time_step * force_scale * 4.0 / 2048.0 * (1.0 + softening) ** 2

    def lane_sums(c, part):
        return jnp.sum(sum_ref[c, pl.ds(part * LANES, LANES), :].T, axis=0, keepdims=True)

    for part in range(atom_rows):
        mass = motion_ref[pl.ds(3 * atom_rows + part, 1), :]
        for c in range(3):
            speed = motion_ref[pl.ds(c * atom_rows + part, 1), :]
            moved = time_step * speed + scale * lane_sums(c, part) * mass
            for copy in range(copies):
                out_ref[pl.ds(copy * rows.disp_count + c * atom_rows + part, 1), :] = moved
    slot = lax.broadcasted_iota(jnp.int32, (1, LANES), 1)
    for part in range(rows.slot_rows):
        flag = jnp.where(slot + part * LANES < count_ref[0, 0], 1.0, 0.0)
        for copy in range(copies):
            out_ref[pl.ds(copy * rows.disp_count + rows.live + part, 1), :] = flag
    if rows.disp_count > rows.disp_used:
        for copy in range(copies):
            out_ref[pl.ds(copy * rows.disp_count + rows.disp_used, rows.disp_count - rows.disp_used), :] = jnp.zeros(
                (rows.disp_count - rows.disp_used, LANES), jnp.float32
            )


def bond_kernel(rows, domains, strides, around_ref, weight_ref, matrix_ref):
    atom_rows, shell_rows = rows.atom_rows, rows.shell_rows

    def load(row):
        return around_ref[pl.ds(row, domains, stride=rows.count), :]

    def index(row):
        return load(row).astype(jnp.int32)

    fields = [[load(at + part) for part in range(atom_rows)] for at in rows.coords + [rows.mass]]

    def weights(first, second, row):
        gap = [first[c] - second[c] for c in range(3)]
        length_sq = gap[0] * gap[0] + gap[1] * gap[1] + gap[2] * gap[2] + length_floor
        scale = lax.rsqrt(length_sq) * lax.rsqrt(first[3] + second[3])
        return [gap[c] * scale for c in range(3)]

    at = 0
    for part in range(rows.bond_rows):
        first = index(rows.bond_first + part)
        second = index(rows.bond_second + part)
        values = weights([pick(f, first) for f in fields], [pick(f, second) for f in fields], at)
        for c in range(3):
            weight_ref[pl.ds((at * 3 + c) * domains, domains), :] = values[c]
        at += 1
    for part in range(rows.slot_rows):
        first = index(rows.cross_first + part)
        second = index(rows.cross_second + part)
        side = load(rows.side + part)
        other = [jnp.zeros((domains, LANES), jnp.float32) for _ in range(4)]
        for code, stride in enumerate(strides):
            seen = pltpu.roll(second, stride % domains, 0)
            for f in range(4):
                value = pltpu.roll(pick(fields[f][:shell_rows], seen), -stride % domains, 0)
                other[f] = jnp.where(side == code, value, other[f])
        values = weights([pick(f[:shell_rows], first) for f in fields], other, at)
        for c in range(3):
            weight_ref[pl.ds((at * 3 + c) * domains, domains), :] = values[c]
        at += 1

    down = lax.broadcasted_iota(jnp.int32, (SUBLANES, LANES), 0)
    group_rows = 4 * SUBLANES

    kind = jnp.bfloat16 if shell_rows * LANES <= 256 else jnp.float32
    across = lax.broadcasted_iota(jnp.int32, (group_rows, LANES), 1).astype(jnp.float32)
    lanes = [(across + float(block * LANES)).astype(kind) for block in range(shell_rows)]

    def column(row, step, half=0):
        row = jnp.broadcast_to(row, (SUBLANES, LANES))
        groups = [take_lanes(row, down + at) for at in range(step * group_rows, (step + 1) * group_rows, SUBLANES)]
        return (jnp.concatenate(groups, axis=0) - float(half * shell_rows * LANES)).astype(kind)

    def put(at, ends, signs):
        for block in range(shell_rows):
            value = jnp.zeros((group_rows, LANES), kind)
            for end, sign in zip(ends, signs):
                value = jnp.where(end == lanes[block], jnp.full((group_rows, LANES), sign, kind), value)
            matrix_ref[pl.ds(at, group_rows), block * LANES : (block + 1) * LANES] = value.astype(matrix_ref.dtype)

    def build(domain, _):
        start = pl.multiple_of(domain * rows.matrix, LANES)
        for part in range(rows.bond_rows):
            first = around_ref[pl.ds(domain * rows.count + rows.bond_first + part, 1), :]
            second = around_ref[pl.ds(domain * rows.count + rows.bond_second + part, 1), :]
            for step in range(LANES // group_rows):
                for half in range(2):
                    ends = (column(first, step, half), column(second, step, half))
                    put(start + rows.inner_at[half] + part * LANES + step * group_rows, ends, (1.0, -1.0))
        for part in range(rows.slot_rows):
            for row_at, to, sign in (
                (rows.cross_first, rows.cross_at, 1.0),
                (rows.cross_second, rows.far_at, -1.0),
            ):
                row = around_ref[pl.ds(domain * rows.count + row_at + part, 1), :]
                for step in range(LANES // group_rows):
                    put(start + to + part * LANES + step * group_rows, (column(row, step),), (sign,))
        return 0

    lax.fori_loop(0, domains, build, 0)


def solve_kernel(
    rows,
    domains,
    strides,
    around_ref,
    moves_ref,
    weight_ref,
    matrix_ref,
    coords_out_ref,
    velocity_out_ref,
    push_ref,
    far_push_ref,
    field_ref,
):
    atom_rows, shell_rows = rows.atom_rows, rows.shell_rows
    bond_rows, slot_rows = rows.bond_rows, rows.slot_rows
    me = place_of()

    def load(row):
        return around_ref[pl.ds(row, domains, stride=rows.count), :]

    def index(row):
        return load(row).astype(jnp.int32)

    inner_first = [index(rows.bond_first + p) for p in range(bond_rows)]
    inner_second = [index(rows.bond_second + p) for p in range(bond_rows)]
    cross_first = [index(rows.cross_first + p) for p in range(slot_rows)]
    cross_second = [index(rows.cross_second + p) for p in range(slot_rows)]
    sides = [load(rows.side + p) for p in range(slot_rows)]
    masses = [load(rows.mass + p) for p in range(atom_rows)]

    def move_rows(row):
        return moves_ref[pl.ds(row, domains, stride=rows.disp_count), :]

    def weight(at, c):
        value = weight_ref[pl.ds((at * 3 + c) * domains, domains), :]
        return value if at < bond_rows else value * live[at - bond_rows]

    live = [move_rows(rows.live + p) for p in range(slot_rows)]

    def project(fields):
        result = []
        for part in range(bond_rows):
            total = 0.0
            for c in range(3):
                ends = pick(fields[c], inner_first[part]) - pick(fields[c], inner_second[part])
                total = total + weight(part, c) * ends
            result.append(total)
        for part in range(slot_rows):
            seen = [pltpu.roll(cross_second[part], stride % domains, 0) for stride in strides]
            total = 0.0
            for c in range(3):
                shell = fields[c][:shell_rows]
                other = 0.0
                for code, stride in enumerate(strides):
                    value = pltpu.roll(pick(shell, seen[code]), -stride % domains, 0)
                    other = jnp.where(sides[part] == code, value, other)
                total = total + weight(bond_rows + part, c) * (pick(shell, cross_first[part]) - other)
            result.append(total)
        return result

    def put_pushes(values):
        for at, value in enumerate(values):
            for c in range(3):
                pushed = weight(at, c) * value
                high = pushed.astype(jnp.bfloat16).astype(jnp.float32)
                for row, part in ((c, high), (3 + c, pushed - high)):
                    push_ref[at, pl.ds(row * domains, domains), :] = part
                    if at >= bond_rows:
                        for code in range(4):
                            far_push_ref[at - bond_rows, pl.ds((code * SUBLANES + row) * domains, domains), :] = (
                                jnp.where(sides[at - bond_rows] == code, part, 0.0)
                            )

    def pushes_of(at, domain):
        return push_ref[at, pl.ds(domain, SUBLANES, stride=domains), :].astype(jnp.bfloat16)

    def product(pushes, domain, at):
        start = domain * rows.matrix + at
        if not isinstance(start, int):
            start = pl.multiple_of(start, LANES)
        pushes = pushes[0] if len(pushes) == 1 else jnp.concatenate(pushes, axis=1)
        result = jnp.dot(
            pushes, matrix_ref[pl.ds(start, pushes.shape[1]), :], preferred_element_type=jnp.float32
        )
        return [result[:, p * LANES : (p + 1) * LANES] for p in range(shell_rows)]

    def inner_totals(domain):
        pushes = [pushes_of(at, domain) for at in range(bond_rows + slot_rows)]
        return product(pushes, domain, 0) + product(pushes[:bond_rows], domain, rows.shell_terms)

    def far_totals(domain, first_row, count):
        pushes = [
            far_push_ref[p, pl.ds(first_row * domains + domain, count, stride=domains), :].astype(jnp.bfloat16)
            for p in range(slot_rows)
        ]
        return product(pushes, domain, rows.far_at)

    def spread(values):
        put_pushes(values)
        for domain in range(domains):
            for part, total in enumerate(inner_totals(domain)):
                field_ref[0, part, pl.ds(domain, SUBLANES, stride=domains), :] = total
            for part, total in enumerate(far_totals(domain, 0, 4 * SUBLANES)):
                for code, stride in enumerate(strides):
                    field_ref[1 + code, part, pl.ds((domain + stride) % domains, SUBLANES, stride=domains), :] = total[
                        code * SUBLANES : (code + 1) * SUBLANES, :
                    ]

        def field(c, part):
            pieces = [
                field_ref[source, part, pl.ds(row * domains, domains), :]
                for source in range(5 if part < shell_rows else 1)
                for row in (c, 3 + c)
            ]
            return masses[part] * functools.reduce(lambda a, b: a + b, pieces)

        return [[field(c, part) for part in range(atom_rows)] for c in range(3)]

    moves = [
        [move_rows(c * atom_rows + p) for p in range(atom_rows)]
        for c in range(3)
    ]
    push_ref[...] = jnp.zeros(push_ref.shape, jnp.float32)
    far_push_ref[...] = jnp.zeros(far_push_ref.shape, jnp.float32)
    residue = project(moves)

    def expand(_, carry):
        residue, summed = carry
        change = project(spread(residue))
        residue = [now - step for now, step in zip(residue, change)]
        return residue, [a + b for a, b in zip(summed, residue)]

    residue, summed = lax.fori_loop(0, ORDER, expand, (residue, residue))
    put_pushes(summed)
    sums = inner_totals(me)
    for code, stride in enumerate(strides):
        owner = lax.rem(me + (-stride) % domains, domains)
        for part, total in enumerate(far_totals(owner, code * SUBLANES, SUBLANES)):
            sums[part] = sums[part] + total
    for part in range(atom_rows):
        lanes = slice(part * LANES, (part + 1) * LANES)
        mass = around_ref[pl.ds(me * rows.count + rows.mass + part, 1), :]
        for c in range(3):
            correction = mass * (sums[part][c : c + 1, :] + sums[part][3 + c : 4 + c, :])
            move = moves_ref[pl.ds(me * rows.disp_count + c * atom_rows + part, 1), :] - correction
            start = around_ref[pl.ds(me * rows.count + rows.coords[c] + part, 1), :]
            coords_out_ref[c, 0, :, lanes] = start + move
            velocity_out_ref[c, 0, :, lanes] = move * (1.0 / time_step)


def vmem(count):
    return [pl.BlockSpec(memory_space=pltpu.VMEM)] * count


def smem(count):
    return [pl.BlockSpec(memory_space=pltpu.SMEM)] * count


def hbm(count):
    return [pl.BlockSpec(memory_space=pltpu.HBM)] * count


def in_hbm(arrays):
    return [pltpu.with_memory_space_constraint(a, pltpu.HBM) for a in arrays]


def params(mebibytes):
    return pltpu.CompilerParams(vmem_limit_bytes=mebibytes * 1024 * 1024)


def cost(flops, moved):
    return pl.CostEstimate(flops=flops, bytes_accessed=moved, transcendentals=0)


def room_for(arrays):
    return [pltpu.VMEM(a.shape, a.dtype) for a in arrays]


def shards(
    coords,
    velocity,
    charge,
    inv_mass,
    tile_block,
    tile_atoms,
    active_tile_count,
    bond_atoms,
    cross_atoms,
    cross_side,
    cross_count,
):
    atoms = coords.shape[-1]
    tiles = tile_atoms.shape[2]
    domains = lax.axis_size("dom")
    strides = strides_of(domains)
    rows = Rows(atoms, bond_atoms.shape[-1], cross_side.shape[-1])
    whole_slab = domains == SUBLANES
    copies = domains if whole_slab else 1
    f32 = jnp.float32

    sent = (coords, charge, inv_mass, bond_atoms, cross_atoms, cross_side)
    packed, rim = pl.pallas_call(
        functools.partial(pack_kernel, rows, copies),
        out_shape=(
            jax.ShapeDtypeStruct((copies * rows.count, LANES), f32),
            jax.ShapeDtypeStruct((4 * rows.shell_rows, LANES), f32),
        ),
        in_specs=hbm(len(sent)),
        out_specs=tuple(vmem(2)),
        scratch_shapes=room_for(sent) + [pltpu.SemaphoreType.DMA((len(sent),))],
        compiler_params=params(4),
        name="pack",
    )(*in_hbm(sent))

    alone = (coords, charge, velocity, inv_mass, tile_atoms)
    own = pl.pallas_call(
        functools.partial(own_kernel, rows),
        out_shape=(
            jax.ShapeDtypeStruct((4, atoms, LANES), f32),
            jax.ShapeDtypeStruct((4, tiles, TILE), f32),
            jax.ShapeDtypeStruct((tiles, TILE), jnp.int32),
            jax.ShapeDtypeStruct((4 * rows.atom_rows, LANES), f32),
        ),
        in_specs=hbm(len(alone)),
        out_specs=tuple(vmem(4)),
        scratch_shapes=room_for(alone[:4]) + [pltpu.SemaphoreType.DMA((len(alone),))],
        compiler_params=params(4),
        cost_estimate=cost(64 * atoms * LANES, 16 * atoms * LANES),
        name="own",
    )(*in_hbm(alone))

    below = passed_along(rim, "slab", 1)
    above = passed_along(rim, "slab", -1)
    if whole_slab:
        around = from_slab(packed)

        def place():
            return [place_of(stride) for stride in strides]

    else:
        around = jnp.concatenate([packed] + [passed_along(packed, "dom", -stride) for stride in strides], axis=0)

        def place():
            return [1, 2, 3, 4]


    moves = pl.pallas_call(
        functools.partial(force_kernel, rows, copies, place),
        out_shape=jax.ShapeDtypeStruct((copies * rows.disp_count, LANES), f32),
        in_specs=smem(2) + hbm(1) + vmem(7),
        out_specs=vmem(1)[0],
        scratch_shapes=[
            pltpu.VMEM((4, 6 * rows.shell_rows, SUBLANES, LANES), f32),
            pltpu.VMEM((4, tiles, LANES), f32),
            pltpu.VMEM((3, atoms, LANES), f32),
            pltpu.SMEM(tile_block.shape, jnp.int32),
            pltpu.SemaphoreType.DMA(()),
        ],
        compiler_params=params(8),
        cost_estimate=cost(30 * tiles * TILE * TILE, 4 * around.size),
        name="force",
    )(active_tile_count, cross_count, *in_hbm([tile_block]), around, below, above, *own)

    if not whole_slab:
        return by_exchange(rows, strides, around, moves, cross_count)

    constraint_rows = rows.bond_rows + rows.slot_rows
    weight, matrix = pl.pallas_call(
        functools.partial(bond_kernel, rows, domains, strides),
        out_shape=(
            jax.ShapeDtypeStruct((constraint_rows * 3 * domains, LANES), f32),
            jax.ShapeDtypeStruct((domains * rows.matrix, atoms // 2), jnp.bfloat16),
        ),
        in_specs=vmem(1),
        out_specs=tuple(vmem(2)),
        compiler_params=params(16),
        cost_estimate=cost(8 * domains * rows.matrix * atoms // 2, 4 * around.size),
        name="bonds",
    )(around)

    every_move = from_slab(moves)

    return pl.pallas_call(
        functools.partial(solve_kernel, rows, domains, strides),
        out_shape=(
            jax.ShapeDtypeStruct(coords.shape, f32),
            jax.ShapeDtypeStruct(coords.shape, f32),
        ),
        in_specs=vmem(4),
        out_specs=tuple(vmem(2)),
        scratch_shapes=[
            pltpu.VMEM((constraint_rows, SUBLANES * domains, LANES), f32),
            pltpu.VMEM((rows.slot_rows, 4 * SUBLANES * domains, LANES), f32),
            pltpu.VMEM((5, rows.atom_rows, SUBLANES * domains, LANES), f32),
        ],
        compiler_params=params(16),
        name="solve",
    )(around, every_move, weight, matrix)


def by_exchange(rows, strides, around, moves, cross_count):
    atom_count = rows.atom_rows * LANES
    shell = rows.shell_rows * LANES
    inside = around.reshape(5, rows.count, LANES)

    def flat(at, count):
        return inside[0, at : at + count].reshape(-1)

    def neighbours(at):
        return inside[1:, at : at + rows.shell_rows].reshape(-1)

    coords = jnp.stack([flat(at, rows.atom_rows) for at in rows.coords])
    inv_mass = flat(rows.mass, rows.atom_rows)
    displace = moves[: rows.live].reshape(3, atom_count)
    left = flat(rows.bond_first, rows.bond_rows).astype(jnp.int32)
    right = flat(rows.bond_second, rows.bond_rows).astype(jnp.int32)
    cross_left = flat(rows.cross_first, rows.slot_rows).astype(jnp.int32)
    cross_right = flat(rows.cross_second, rows.slot_rows).astype(jnp.int32)
    side = flat(rows.side, rows.slot_rows).astype(jnp.int32)
    flag = moves[rows.live : rows.disp_used].reshape(-1)
    cross_index = side * shell + cross_right
    far_coords = jnp.stack([neighbours(at) for at in rows.coords])
    far_mass = neighbours(rows.mass)

    def weights(first, second, mass_first, mass_second):
        gap = first - second
        length = jnp.sqrt(jnp.sum(gap * gap, axis=0) + length_floor)
        return gap / length * lax.rsqrt(mass_first + mass_second)

    inner = weights(coords[:, left], coords[:, right], inv_mass[left], inv_mass[right])
    cross = flag * weights(
        coords[:, cross_left], far_coords[:, cross_index], inv_mass[cross_left], far_mass[cross_index]
    )

    def project(field):
        rim = field[:, :shell]
        far = jnp.concatenate([passed_along(rim, "dom", -stride) for stride in strides], axis=1)
        return (
            jnp.sum(inner * (field[:, left] - field[:, right]), axis=0),
            jnp.sum(cross * (field[:, cross_left] - far[:, cross_index]), axis=0),
        )

    def spread(values):
        pushed = inner * values[0]
        pushed_cross = cross * values[1]
        totals = jnp.zeros((3, atom_count), jnp.float32).at[:, left].add(pushed).at[:, right].add(-pushed)
        totals = totals.at[:, cross_left].add(pushed_cross)
        outward = jnp.zeros((3, 4 * shell), jnp.float32).at[:, cross_index].add(-pushed_cross)
        for code, stride in enumerate(strides):
            totals = totals.at[:, :shell].add(
                passed_along(outward[:, code * shell : (code + 1) * shell], "dom", stride)
            )
        return inv_mass * totals

    residue = project(displace)
    summed = residue
    for _ in range(ORDER):
        change = project(spread(residue))
        residue = tuple(now - step for now, step in zip(residue, change))
        summed = tuple(a + b for a, b in zip(summed, residue))
    move = displace - spread(summed)
    return (
        (coords + move).reshape(3, 1, 1, atom_count),
        (move * (1.0 / time_step)).reshape(3, 1, 1, atom_count),
    )


def solution(mesh):
    return jax.shard_map(
        shards,
        mesh=mesh,
        in_specs=(
            P(None, "slab", "dom", None),
            P(None, "slab", "dom", None),
            P("slab", "dom", None),
            P("slab", "dom", None),
            P("slab", "dom", None),
            P("slab", "dom", None, None),
            P("slab", "dom"),
            P(None, "slab", "dom", None),
            P(None, "slab", "dom", None),
            P("slab", "dom", None),
            P("slab", "dom"),
        ),
        out_specs=(P(None, "slab", "dom", None), P(None, "slab", "dom", None)),
        check_vma=False,
    )
```

profile of v0, /device:TPU:0, one launch (start us, length us, event | category | flops | bytes accessed | tf_op | source)
XLA Modules:
  0.0 32.6 jit_solution(7674443026899212014)
XLA Ops:
  0.6 1.5 %pack.1 = (f32[256,128]{1,0:T(8,128)}, f32[8,128]{1,0:T(8,128)S(1)}) custom-call(f32[3,1,1,512]{3,2,1,0:T(1,128)} %coords_hbm.1, f32[1,1,512]{2,1,0:T(1,128)} %charge_hbm.1, f32[1,1,512]{2,1,0:T(1,128)} %mass_hbm.1, s32[2,1,1,256]{3,2,1,0:T(1,128)} %refs_3_.1, s32[2,1,1,128]{3,2,1,0:T(1,128)} %refs_4_.1, s32[1,1,128]{2,1,0:T(1,128)} %refs_5_.1), custom_call_target="tpu_custom_call" | custom-call | tf_op jit(solution)/shard_map/pack/pallas_call | solution.py:593
  2.2 9.3 %all-to-all-start = ((f32[8,32,128]{2,1,0:T(8,128)}), f32[8,32,128]{2,1,0:T(8,128)S(1)}, u32[]{:S(2)}, u32[]{:S(2)}) async-start(f32[8,32,128]{2,1,0:T(8,128)} %bitcast), calls=%async_computation | async-start | bytes 262144 | tf_op jit(solution)/shard_map/all_to_all | solution.py:33
  11.4 0.7 %collective-permute-start.1 = (f32[8,128]{1,0:T(8,128)S(1)}, f32[8,128]{1,0:T(8,128)S(1)}, u32[]{:S(2)}, u32[]{:S(2)}) collective-permute-start(f32[8,128]{1,0:T(8,128)S(1)} %get-tuple-element.11), channel_id=1, source_target_pairs={{0,24},{8,0},{16,8},{24,16},{1,25},{9,1},{17,9},{25,17},{2,26},{10... | collective-permute-start | bytes 12296 | tf_op jit(solution)/shard_map/ppermute | solution.py:23
  12.1 0.0 collective-permute-start
  13.4 1.5 %own.1 = (f32[4,512,128]{2,1,0:T(8,128)S(1)}, f32[4,64,128]{2,1,0:T(8,128)S(1)}, s32[64,128]{1,0:T(8,128)S(1)}, f32[16,128]{1,0:T(8,128)S(1)}) custom-call(f32[3,1,1,512]{3,2,1,0:T(1,128)} %coords_hbm.1, f32[1,1,512]{2,1,0:T(1,128)} %charge_hbm.1, f32[3,1,1,512]{3,2,1,0:T(1,128)} %velocity_hbm.1, f32[1,1,512]{2,1,0:T(1,128)} %mass_hbm.1, ...), custom_call_target="tpu_custom_call" | custom-call | flops 4194304 | bytes 1048576 | tf_op jit(solution)/shard_map/own/pallas_call | solution.py:607
  14.9 0.0 collective-permute-done.1.above_ref
  14.9 0.2 collective-permute-done.below_ref
  15.1 0.3 all-to-all-done
  15.4 4.0 %force.1 = f32[128,128]{1,0:T(8,128)} custom-call(s32[1,1]{1,0:T(1,128)S(6)} %copy.13.live_ref, s32[1,1]{1,0:T(1,128)S(6)} %copy.14.count_ref, s32[1,1,64]{2,1,0:T(1,128)} %block_hbm.1, f32[256,128]{1,0:T(8,128)S(1)} %bitcast.4, f32[8,128]{1,0:T(8,128)S(1)} %collective-permute-done.below_ref, f32[8,128]{1,0:T(8,128)S(1)} %collective-permute-done.1.above_ref, ...), custom_call_target="tpu_custom_call" | custom-call | flops 31457280 | bytes 131072 | tf_op jit(solution)/shard_map/force/pallas_call | solution.py:638
  19.5 6.0 %all-to-all-start.1 = ((f32[8,16,128]{2,1,0:T(8,128)}), f32[8,16,128]{2,1,0:T(8,128)S(1)}, u32[]{:S(2)}, u32[]{:S(2)}) async-start(f32[8,16,128]{2,1,0:T(8,128)} %bitcast.2), calls=%async_computation.1 | async-start | bytes 131072 | tf_op jit(solution)/shard_map/all_to_all | solution.py:33
  25.5 2.7 %bonds.1 = (f32[72,128]{1,0:T(8,128)S(1)}, bf16[6144,256]{1,0:T(8,128)(2,1)S(1)}) custom-call(f32[256,128]{1,0:T(8,128)S(1)} %bitcast.5), custom_call_target="tpu_custom_call" | custom-call | flops 12582912 | bytes 131072 | tf_op jit(solution)/shard_map/bonds/pallas_call | solution.py:659
  28.2 0.3 %all-to-all-done.1 = f32[8,16,128]{2,1,0:T(8,128)S(1)} async-done(((f32[8,16,128]{2,1,0:T(8,128)}), f32[8,16,128]{2,1,0:T(8,128)S(1)}, u32[]{:S(2)}, u32[]{:S(2)}) %all-to-all-start.1) | async-done | bytes 65568 | tf_op jit(solution)/shard_map/all_to_all | solution.py:33
  28.5 4.1 %solve.1 = (f32[3,1,1,512]{3,2,1,0:T(1,128)}, f32[3,1,1,512]{3,2,1,0:T(1,128)}) custom-call(f32[256,128]{1,0:T(8,128)S(1)} %bitcast.6, f32[128,128]{1,0:T(8,128)S(1)} %bitcast.7, f32[72,128]{1,0:T(8,128)S(1)} %get-tuple-element.16.weight_ref, bf16[6144,256]{1,0:T(8,128)(2,1)S(1)} %get-tuple-element.17.matrix_ref), custom_call_target="tpu_custom_call" | custom-call | tf_op jit(solution)/shard_map/solve/pallas_call | solution.py:674
Async XLA Ops:
  2.2 13.3 %all-to-all-start = ((f32[8,32,128]{2,1,0:T(8,128)}), f32[8,32,128]{2,1,0:T(8,128)S(1)}, u32[]{:S(2)}, u32[]{:S(2)}) async-start(f32[8,32,128]{2,1,0:T(8,128)} %bitcast), calls=%async_computation | async-start | bytes 262144 | tf_op jit(solution)/shard_map/all_to_all | solution.py:33
  11.4 3.5 %collective-permute-start.1 = (f32[8,128]{1,0:T(8,128)S(1)}, f32[8,128]{1,0:T(8,128)S(1)}, u32[]{:S(2)}, u32[]{:S(2)}) collective-permute-start(f32[8,128]{1,0:T(8,128)S(1)} %get-tuple-element.11), channel_id=1, source_target_pairs={{0,24},{8,0},{16,8},{24,16},{1,25},{9,1},{17,9},{25,17},{2,26},{10... | collective-permute-start | bytes 12296 | tf_op jit(solution)/shard_map/ppermute | solution.py:23
  12.1 3.0 %collective-permute-start = (f32[8,128]{1,0:T(8,128)S(1)}, f32[8,128]{1,0:T(8,128)S(1)}, u32[]{:S(2)}, u32[]{:S(2)}) collective-permute-start(f32[8,128]{1,0:T(8,128)S(1)} %get-tuple-element.11), channel_id=1, source_target_pairs={{0,8},{8,16},{16,24},{24,0},{1,9},{9,17},{17,25},{25,1},{2,10},{10... | collective-permute-start | bytes 12296 | tf_op jit(solution)/shard_map/ppermute | solution.py:23
  19.5 9.0 %all-to-all-start.1 = ((f32[8,16,128]{2,1,0:T(8,128)}), f32[8,16,128]{2,1,0:T(8,128)S(1)}, u32[]{:S(2)}, u32[]{:S(2)}) async-start(f32[8,16,128]{2,1,0:T(8,128)} %bitcast.2), calls=%async_computation.1 | async-start | bytes 131072 | tf_op jit(solution)/shard_map/all_to_all | solution.py:33
where the time goes:
time: 33.2 us; the launch traced here: 32.6 us
  starting transfers between devices  15.9 us (48%)
  Pallas kernels  13.9 us (42%)
  between operations  1.97 us (6%)
  waiting for transfers between devices  0.85 us (3%)
    all_to_all x2, starting transfers between devices, from_slab(): lax.all_to_all(blocks, 'dom', 0, 0, axis_index_groups=[order], tiled=True)  15.3 us
    pallas_call x1, Pallas kernels, shards(): pl.pallas_call(functools.partial(solve_kernel, rows, domains, strides), o...  4.12 us
    pallas_call x1, Pallas kernels, shards(): pl.pallas_call(functools.partial(force_kernel, rows, copies, place), out_...  4.03 us
    pallas_call x1, Pallas kernels, shards(): pl.pallas_call(functools.partial(bond_kernel, rows, domains, strides), ou...  2.66 us
    pallas_call x1, Pallas kernels, shards(): pl.pallas_call(functools.partial(own_kernel, rows), out_shape=(jax.ShapeD...  1.53 us
    pallas_call x1, Pallas kernels, shards(): pl.pallas_call(functools.partial(pack_kernel, rows, copies), out_shape=(j...  1.51 us
    all_to_all x2, waiting for transfers between devices, from_slab(): lax.all_to_all(blocks, 'dom', 0, 0, axis_index_groups=[order], tiled=True)  0.67 us
  transfers between devices with their start and end apart: 4, of which 3 were waited for; matrix products, arithmetic and copies ran while one was open for 0% of the time, Pallas kernels for 13%

commit v1 on v0

--- a/solution.py
+++ b/solution.py
@@ -59,7 +59,7 @@
             self.coords.append(at)
             at += self.atom_rows
         self.charge = at
-        at += self.atom_rows
+        at += self.shell_rows
         self.mass = at
         at += self.atom_rows
         self.bond_first = at
@@ -70,8 +70,6 @@
         at += self.slot_rows
         self.cross_second = at
         at += self.slot_rows
-        self.side = at
-        at += self.slot_rows
         self.used = at
         self.count = round_up(at, SUBLANES)
         self.shell_terms = (self.bond_rows + self.slot_rows) * LANES
@@ -80,7 +78,8 @@
         self.far_at = self.shell_terms + self.bond_rows * LANES
         self.matrix = self.far_at + self.slot_rows * LANES
         self.live = 3 * self.atom_rows
-        self.disp_used = self.live + self.slot_rows
+        self.side = self.live + self.slot_rows
+        self.disp_used = self.side + self.slot_rows
         self.disp_count = round_up(self.disp_used, SUBLANES)
 
 
@@ -105,10 +104,10 @@
 
 
 def pack_kernel(rows, copies, *refs):
-    sources, (out_ref, rim_ref), targets, sem_ref = refs[:6], refs[6:8], refs[8:14], refs[14]
+    sources, (out_ref, rim_ref), targets, sem_ref = refs[:5], refs[5:7], refs[7:12], refs[12]
     for copy in fetched(sources, targets, sem_ref):
         copy.wait()
-    coords_ref, charge_ref, mass_ref, bonds_ref, cross_ref, side_ref = targets
+    coords_ref, charge_ref, mass_ref, bonds_ref, cross_ref = targets
 
     def put(row, value):
         for part in range(value.shape[1] // LANES):
@@ -117,7 +116,7 @@
                 out_ref[pl.ds(copy * rows.count + row + part, 1), :] = piece
 
     shell = rows.shell_rows * LANES
-    fields = [coords_ref[c, 0] for c in range(3)] + [charge_ref[0]]
+    fields = [coords_ref[c, 0] for c in range(3)] + [charge_ref[0, :, :shell]]
     for c in range(4):
         at = rows.coords[c] if c < 3 else rows.charge
         put(at, fields[c])
@@ -128,7 +127,6 @@
     put(rows.bond_second, bonds_ref[1, 0].astype(jnp.float32))
     put(rows.cross_first, cross_ref[0, 0].astype(jnp.float32))
     put(rows.cross_second, cross_ref[1, 0].astype(jnp.float32))
-    put(rows.side, side_ref[0].astype(jnp.float32))
     if rows.count > rows.used:
         for copy in range(copies):
             out_ref[pl.ds(copy * rows.count + rows.used, rows.count - rows.used), :] = jnp.zeros(
@@ -148,6 +146,7 @@
     charge_hbm,
     velocity_hbm,
     mass_hbm,
+    side_hbm,
     atoms_hbm,
     own_ref,
     far_ref,
@@ -157,12 +156,13 @@
     charge_ref,
     velocity_ref,
     mass_ref,
+    side_ref,
     sem_ref,
 ):
     atom_rows = rows.atom_rows
     copies = fetched(
-        (coords_hbm, charge_hbm, atoms_hbm.at[0, 0], velocity_hbm, mass_hbm),
-        (coords_ref, charge_ref, index_ref, velocity_ref, mass_ref),
+        (coords_hbm, charge_hbm, atoms_hbm.at[0, 0], velocity_hbm, mass_hbm, side_hbm),
+        (coords_ref, charge_ref, index_ref, velocity_ref, mass_ref, side_ref),
         sem_ref,
     )
     down = lax.broadcasted_iota(jnp.int32, (SUBLANES, LANES), 0)
@@ -190,12 +190,14 @@
         index = index_ref[at, :]
         for c in range(4):
             far_ref[c, at, :] = pick(table[c], index)
-    copies[3].wait()
-    copies[4].wait()
-    fields = [velocity_ref[c, 0] for c in range(3)] + [mass_ref[0]]
-    for c, field in enumerate(fields):
-        for part in range(atom_rows):
-            motion_ref[pl.ds(c * atom_rows + part, 1), :] = field[:, lanes_of(part)]
+    for copy in copies[3:]:
+        copy.wait()
+    fields = [velocity_ref[c, 0] for c in range(3)] + [mass_ref[0], side_ref[0].astype(jnp.float32)]
+    at = 0
+    for field in fields:
+        for part in range(field.shape[1] // LANES):
+            motion_ref[pl.ds(at, 1), :] = field[:, lanes_of(part)]
+            at += 1
 
 
 def force_kernel(
@@ -285,21 +287,24 @@
 
     scale = time_step * time_step * force_scale * 4.0 / 2048.0 * (1.0 + softening) ** 2
 
-    def lane_sums(c, part):
-        return jnp.sum(sum_ref[c, pl.ds(part * LANES, LANES), :].T, axis=0, keepdims=True)
-
-    for part in range(atom_rows):
-        mass = motion_ref[pl.ds(3 * atom_rows + part, 1), :]
-        for c in range(3):
-            speed = motion_ref[pl.ds(c * atom_rows + part, 1), :]
-            moved = time_step * speed + scale * lane_sums(c, part) * mass
-            for copy in range(copies):
-                out_ref[pl.ds(copy * rows.disp_count + c * atom_rows + part, 1), :] = moved
+    lane = lax.broadcasted_iota(jnp.int32, (LANES, LANES), 1)
+    columns = jnp.zeros((LANES, LANES), jnp.float32)
+    for c in range(3):
+        for part in range(atom_rows):
+            total = jnp.sum(sum_ref[c, pl.ds(part * LANES, LANES), :], axis=1, keepdims=True)
+            columns = jnp.where(lane == c * atom_rows + part, total, columns)
+    totals = columns.T[: 3 * atom_rows, :]
+    mass = motion_ref[pl.ds(3 * atom_rows, atom_rows), :]
+    moved = time_step * motion_ref[pl.ds(0, 3 * atom_rows), :] + scale * totals * jnp.concatenate([mass] * 3, axis=0)
+    for copy in range(copies):
+        out_ref[pl.ds(copy * rows.disp_count, 3 * atom_rows), :] = moved
     slot = lax.broadcasted_iota(jnp.int32, (1, LANES), 1)
     for part in range(rows.slot_rows):
         flag = jnp.where(slot + part * LANES < count_ref[0, 0], 1.0, 0.0)
+        side = motion_ref[pl.ds(4 * atom_rows + part, 1), :]
         for copy in range(copies):
             out_ref[pl.ds(copy * rows.disp_count + rows.live + part, 1), :] = flag
+            out_ref[pl.ds(copy * rows.disp_count + rows.side + part, 1), :] = side
     if rows.disp_count > rows.disp_used:
         for copy in range(copies):
             out_ref[pl.ds(copy * rows.disp_count + rows.disp_used, rows.disp_count - rows.disp_used), :] = jnp.zeros(
@@ -318,34 +323,26 @@
 
     fields = [[load(at + part) for part in range(atom_rows)] for at in rows.coords + [rows.mass]]
 
-    def weights(first, second, row):
+    def put_weights(first, second, at):
         gap = [first[c] - second[c] for c in range(3)]
         length_sq = gap[0] * gap[0] + gap[1] * gap[1] + gap[2] * gap[2] + length_floor
         scale = lax.rsqrt(length_sq) * lax.rsqrt(first[3] + second[3])
-        return [gap[c] * scale for c in range(3)]
-
-    at = 0
+        for c in range(3):
+            weight_ref[pl.ds((at * 3 + c) * domains, domains), :] = gap[c] * scale
+
     for part in range(rows.bond_rows):
         first = index(rows.bond_first + part)
         second = index(rows.bond_second + part)
-        values = weights([pick(f, first) for f in fields], [pick(f, second) for f in fields], at)
-        for c in range(3):
-            weight_ref[pl.ds((at * 3 + c) * domains, domains), :] = values[c]
-        at += 1
+        put_weights([pick(f, first) for f in fields], [pick(f, second) for f in fields], part)
+    shells = [f[:shell_rows] for f in fields]
     for part in range(rows.slot_rows):
         first = index(rows.cross_first + part)
         second = index(rows.cross_second + part)
-        side = load(rows.side + part)
-        other = [jnp.zeros((domains, LANES), jnp.float32) for _ in range(4)]
+        ends = [pick(f, first) for f in shells]
         for code, stride in enumerate(strides):
             seen = pltpu.roll(second, stride % domains, 0)
-            for f in range(4):
-                value = pltpu.roll(pick(fields[f][:shell_rows], seen), -stride % domains, 0)
-                other[f] = jnp.where(side == code, value, other[f])
-        values = weights([pick(f[:shell_rows], first) for f in fields], other, at)
-        for c in range(3):
-            weight_ref[pl.ds((at * 3 + c) * domains, domains), :] = values[c]
-        at += 1
+            others = [pltpu.roll(pick(f, seen), -stride % domains, 0) for f in shells]
+            put_weights(ends, others, rows.bond_rows + part * 4 + code)
 
     down = lax.broadcasted_iota(jnp.int32, (SUBLANES, LANES), 0)
     group_rows = 4 * SUBLANES
@@ -416,17 +413,26 @@
     inner_second = [index(rows.bond_second + p) for p in range(bond_rows)]
     cross_first = [index(rows.cross_first + p) for p in range(slot_rows)]
     cross_second = [index(rows.cross_second + p) for p in range(slot_rows)]
-    sides = [load(rows.side + p) for p in range(slot_rows)]
     masses = [load(rows.mass + p) for p in range(atom_rows)]
 
     def move_rows(row):
         return moves_ref[pl.ds(row, domains, stride=rows.disp_count), :]
 
+    def weight_rows(at, c):
+        return weight_ref[pl.ds((at * 3 + c) * domains, domains), :]
+
+    sides = [move_rows(rows.side + p) for p in range(slot_rows)]
+    cross_weights = []
+    for part in range(slot_rows):
+        live = move_rows(rows.live + part)
+        for c in range(3):
+            value = 0.0
+            for code in range(4):
+                value = jnp.where(sides[part] == code, weight_rows(bond_rows + part * 4 + code, c), value)
+            cross_weights.append(value * live)
+
     def weight(at, c):
-        value = weight_ref[pl.ds((at * 3 + c) * domains, domains), :]
-        return value if at < bond_rows else value * live[at - bond_rows]
-
-    live = [move_rows(rows.live + p) for p in range(slot_rows)]
+        return weight_rows(at, c) if at < bond_rows else cross_weights[(at - bond_rows) * 3 + c]
 
     def project(fields):
         result = []
@@ -589,7 +595,7 @@
     copies = domains if whole_slab else 1
     f32 = jnp.float32
 
-    sent = (coords, charge, inv_mass, bond_atoms, cross_atoms, cross_side)
+    sent = (coords, charge, inv_mass, bond_atoms, cross_atoms)
     packed, rim = pl.pallas_call(
         functools.partial(pack_kernel, rows, copies),
         out_shape=(
@@ -603,18 +609,18 @@
         name="pack",
     )(*in_hbm(sent))
 
-    alone = (coords, charge, velocity, inv_mass, tile_atoms)
+    alone = (coords, charge, velocity, inv_mass, cross_side, tile_atoms)
     own = pl.pallas_call(
         functools.partial(own_kernel, rows),
         out_shape=(
             jax.ShapeDtypeStruct((4, atoms, LANES), f32),
             jax.ShapeDtypeStruct((4, tiles, TILE), f32),
             jax.ShapeDtypeStruct((tiles, TILE), jnp.int32),
-            jax.ShapeDtypeStruct((4 * rows.atom_rows, LANES), f32),
+            jax.ShapeDtypeStruct((4 * rows.atom_rows + rows.slot_rows, LANES), f32),
         ),
         in_specs=hbm(len(alone)),
         out_specs=tuple(vmem(4)),
-        scratch_shapes=room_for(alone[:4]) + [pltpu.SemaphoreType.DMA((len(alone),))],
+        scratch_shapes=room_for(alone[:5]) + [pltpu.SemaphoreType.DMA((len(alone),))],
         compiler_params=params(4),
         cost_estimate=cost(64 * atoms * LANES, 16 * atoms * LANES),
         name="own",
@@ -659,7 +665,7 @@
     weight, matrix = pl.pallas_call(
         functools.partial(bond_kernel, rows, domains, strides),
         out_shape=(
-            jax.ShapeDtypeStruct((constraint_rows * 3 * domains, LANES), f32),
+            jax.ShapeDtypeStruct(((rows.bond_rows + 4 * rows.slot_rows) * 3 * domains, LANES), f32),
             jax.ShapeDtypeStruct((domains * rows.matrix, atoms // 2), jnp.bfloat16),
         ),
         in_specs=vmem(1),
@@ -707,8 +713,8 @@
     right = flat(rows.bond_second, rows.bond_rows).astype(jnp.int32)
     cross_left = flat(rows.cross_first, rows.slot_rows).astype(jnp.int32)
     cross_right = flat(rows.cross_second, rows.slot_rows).astype(jnp.int32)
-    side = flat(rows.side, rows.slot_rows).astype(jnp.int32)
-    flag = moves[rows.live : rows.disp_used].reshape(-1)
+    side = moves[rows.side : rows.side + rows.slot_rows].reshape(-1).astype(jnp.int32)
+    flag = moves[rows.live : rows.side].reshape(-1)
     cross_index = side * shell + cross_right
     far_coords = jnp.stack([neighbours(at) for at in rows.coords])
     far_mass = neighbours(rows.mass)

time: 33.2 us -> 33 us (level)
  starting transfers between devices: 15.9 us -> 18.1 us
  Pallas kernels: 13.9 us -> 12 us
    all_to_all x2, starting transfers between devices: 15.3 us -> 17.5 us  [from_slab(): lax.all_to_all(blocks, 'dom', 0, 0, axis_index_groups=[order], tiled=True)]
    pallas_call x1, Pallas kernels: 4.03 us -> 2.26 us  [shards(): pl.pallas_call(functools.partial(force_kernel, rows, copies, place), out_...]
  transfers between devices with their start and end apart: 4 -> 4, of which waited for: 3 -> 2; matrix products, arithmetic and copies ran while one was open for 0% -> 0% of each run, Pallas kernels for 13% -> 13%
where the time goes in v1:
time: 33 us; the launch traced here: 32.7 us
  starting transfers between devices  18.1 us (55%)
  Pallas kernels  12 us (36%)
  between operations  1.97 us (6%)
  waiting for transfers between devices  0.55 us (2%)
    all_to_all x2, starting transfers between devices, from_slab(): lax.all_to_all(blocks, 'dom', 0, 0, axis_index_groups=[order], tiled=True)  17.5 us
    pallas_call x1, Pallas kernels, shards(): pl.pallas_call(functools.partial(solve_kernel, rows, domains, strides), o...  4.11 us
    pallas_call x1, Pallas kernels, shards(): pl.pallas_call(functools.partial(bond_kernel, rows, domains, strides), ou...  2.65 us
    pallas_call x1, Pallas kernels, shards(): pl.pallas_call(functools.partial(force_kernel, rows, copies, place), out_...  2.26 us
    pallas_call x1, Pallas kernels, shards(): pl.pallas_call(functools.partial(own_kernel, rows), out_shape=(jax.ShapeD...  1.54 us
    pallas_call x1, Pallas kernels, shards(): pl.pallas_call(functools.partial(pack_kernel, rows, copies), out_shape=(j...  1.47 us
  transfers between devices with their start and end apart: 4, of which 2 were waited for; matrix products, arithmetic and copies ran while one was open for 0% of the time, Pallas kernels for 13%

profile of v1, /device:TPU:0, one launch (start us, length us, event | category | flops | bytes accessed | tf_op | source)
XLA Modules:
  0.0 32.7 jit_solution(7519377240721032533)
XLA Ops:
  0.6 1.5 %pack.1 = (f32[192,128]{1,0:T(8,128)}, f32[8,128]{1,0:T(8,128)S(1)}) custom-call(f32[3,1,1,512]{3,2,1,0:T(1,128)} %coords_hbm.1, f32[1,1,512]{2,1,0:T(1,128)} %charge_hbm.1, f32[1,1,512]{2,1,0:T(1,128)} %mass_hbm.1, s32[2,1,1,256]{3,2,1,0:T(1,128)} %refs_3_.1, s32[2,1,1,128]{3,2,1,0:T(1,128)} %refs_4_.1), custom_call_target="tpu_custom_call" | custom-call | tf_op jit(solution)/shard_map/pack/pallas_call | solution.py:599
  2.1 9.3 %all-to-all-start = ((f32[8,24,128]{2,1,0:T(8,128)}), f32[8,24,128]{2,1,0:T(8,128)S(1)}, u32[]{:S(2)}, u32[]{:S(2)}) async-start(f32[8,24,128]{2,1,0:T(8,128)} %bitcast), calls=%async_computation | async-start | bytes 196608 | tf_op jit(solution)/shard_map/all_to_all | solution.py:33
  11.4 0.7 %collective-permute-start.1 = (f32[8,128]{1,0:T(8,128)S(1)}, f32[8,128]{1,0:T(8,128)S(1)}, u32[]{:S(2)}, u32[]{:S(2)}) collective-permute-start(f32[8,128]{1,0:T(8,128)S(1)} %get-tuple-element.11), channel_id=1, source_target_pairs={{0,24},{8,0},{16,8},{24,16},{1,25},{9,1},{17,9},{25,17},{2,26},{10... | collective-permute-start | bytes 12296 | tf_op jit(solution)/shard_map/ppermute | solution.py:23
  12.0 0.0 collective-permute-start
  13.3 1.5 %own.1 = (f32[4,512,128]{2,1,0:T(8,128)S(1)}, f32[4,64,128]{2,1,0:T(8,128)S(1)}, s32[64,128]{1,0:T(8,128)S(1)}, f32[17,128]{1,0:T(8,128)S(1)}) custom-call(f32[3,1,1,512]{3,2,1,0:T(1,128)} %coords_hbm.1, f32[1,1,512]{2,1,0:T(1,128)} %charge_hbm.1, f32[3,1,1,512]{3,2,1,0:T(1,128)} %velocity_hbm.1, f32[1,1,512]{2,1,0:T(1,128)} %mass_hbm.1, ...), custom_call_target="tpu_custom_call" | custom-call | flops 4194304 | bytes 1048576 | tf_op jit(solution)/shard_map/own/pallas_call | solution.py:613
  14.9 0.0 collective-permute-done.1.above_ref
  14.9 0.2 collective-permute-done.below_ref
  15.1 0.0 all-to-all-done
  15.1 2.3 %force.1 = f32[128,128]{1,0:T(8,128)} custom-call(s32[1,1]{1,0:T(1,128)S(6)} %copy.13.live_ref, s32[1,1]{1,0:T(1,128)S(6)} %copy.14.count_ref, s32[1,1,64]{2,1,0:T(1,128)} %block_hbm.1, f32[192,128]{1,0:T(8,128)S(1)} %bitcast.4, f32[8,128]{1,0:T(8,128)S(1)} %collective-permute-done.below_ref, f32[8,128]{1,0:T(8,128)S(1)} %collective-permute-done.1.above_ref, ...), custom_call_target="tpu_custom_call" | custom-call | flops 31457280 | bytes 98304 | tf_op jit(solution)/shard_map/force/pallas_call | solution.py:644
  17.3 8.2 %all-to-all-start.1 = ((f32[8,16,128]{2,1,0:T(8,128)}), f32[8,16,128]{2,1,0:T(8,128)S(1)}, u32[]{:S(2)}, u32[]{:S(2)}) async-start(f32[8,16,128]{2,1,0:T(8,128)} %bitcast.2), calls=%async_computation.1 | async-start | bytes 131072 | tf_op jit(solution)/shard_map/all_to_all | solution.py:33
  25.5 2.7 %bonds.1 = (f32[144,128]{1,0:T(8,128)S(1)}, bf16[6144,256]{1,0:T(8,128)(2,1)S(1)}) custom-call(f32[192,128]{1,0:T(8,128)S(1)} %bitcast.5), custom_call_target="tpu_custom_call" | custom-call | flops 12582912 | bytes 98304 | tf_op jit(solution)/shard_map/bonds/pallas_call | solution.py:665
  28.2 0.4 %all-to-all-done.1 = f32[8,16,128]{2,1,0:T(8,128)S(1)} async-done(((f32[8,16,128]{2,1,0:T(8,128)}), f32[8,16,128]{2,1,0:T(8,128)S(1)}, u32[]{:S(2)}, u32[]{:S(2)}) %all-to-all-start.1) | async-done | bytes 65568 | tf_op jit(solution)/shard_map/all_to_all | solution.py:33
  28.6 4.1 %solve.1 = (f32[3,1,1,512]{3,2,1,0:T(1,128)}, f32[3,1,1,512]{3,2,1,0:T(1,128)}) custom-call(f32[192,128]{1,0:T(8,128)S(1)} %bitcast.6, f32[128,128]{1,0:T(8,128)S(1)} %bitcast.7, f32[144,128]{1,0:T(8,128)S(1)} %get-tuple-element.16.weight_ref, bf16[6144,256]{1,0:T(8,128)(2,1)S(1)} %get-tuple-element.17.matrix_ref), custom_call_target="tpu_custom_call" | custom-call | tf_op jit(solution)/shard_map/solve/pallas_call | solution.py:680
Async XLA Ops:
  2.1 13.0 %all-to-all-start = ((f32[8,24,128]{2,1,0:T(8,128)}), f32[8,24,128]{2,1,0:T(8,128)S(1)}, u32[]{:S(2)}, u32[]{:S(2)}) async-start(f32[8,24,128]{2,1,0:T(8,128)} %bitcast), calls=%async_computation | async-start | bytes 196608 | tf_op jit(solution)/shard_map/all_to_all | solution.py:33
  11.4 3.5 %collective-permute-start.1 = (f32[8,128]{1,0:T(8,128)S(1)}, f32[8,128]{1,0:T(8,128)S(1)}, u32[]{:S(2)}, u32[]{:S(2)}) collective-permute-start(f32[8,128]{1,0:T(8,128)S(1)} %get-tuple-element.11), channel_id=1, source_target_pairs={{0,24},{8,0},{16,8},{24,16},{1,25},{9,1},{17,9},{25,17},{2,26},{10... | collective-permute-start | bytes 12296 | tf_op jit(solution)/shard_map/ppermute | solution.py:23
  12.0 3.0 %collective-permute-start = (f32[8,128]{1,0:T(8,128)S(1)}, f32[8,128]{1,0:T(8,128)S(1)}, u32[]{:S(2)}, u32[]{:S(2)}) collective-permute-start(f32[8,128]{1,0:T(8,128)S(1)} %get-tuple-element.11), channel_id=1, source_target_pairs={{0,8},{8,16},{16,24},{24,0},{1,9},{9,17},{17,25},{25,1},{2,10},{10... | collective-permute-start | bytes 12296 | tf_op jit(solution)/shard_map/ppermute | solution.py:23
  17.3 11.2 %all-to-all-start.1 = ((f32[8,16,128]{2,1,0:T(8,128)}), f32[8,16,128]{2,1,0:T(8,128)S(1)}, u32[]{:S(2)}, u32[]{:S(2)}) async-start(f32[8,16,128]{2,1,0:T(8,128)} %bitcast.2), calls=%async_computation.1 | async-start | bytes 131072 | tf_op jit(solution)/shard_map/all_to_all | solution.py:33

commit v2 on v1

--- a/solution.py
+++ b/solution.py
@@ -105,15 +105,14 @@
 
 def pack_kernel(rows, copies, *refs):
     sources, (out_ref, rim_ref), targets, sem_ref = refs[:5], refs[5:7], refs[7:12], refs[12]
+    block_ref = refs[13]
     for copy in fetched(sources, targets, sem_ref):
         copy.wait()
     coords_ref, charge_ref, mass_ref, bonds_ref, cross_ref = targets
 
     def put(row, value):
         for part in range(value.shape[1] // LANES):
-            piece = value[:, part * LANES : (part + 1) * LANES]
-            for copy in range(copies):
-                out_ref[pl.ds(copy * rows.count + row + part, 1), :] = piece
+            block_ref[pl.ds(row + part, 1), :] = value[:, part * LANES : (part + 1) * LANES]
 
     shell = rows.shell_rows * LANES
     fields = [coords_ref[c, 0] for c in range(3)] + [charge_ref[0, :, :shell]]
@@ -128,10 +127,10 @@
     put(rows.cross_first, cross_ref[0, 0].astype(jnp.float32))
     put(rows.cross_second, cross_ref[1, 0].astype(jnp.float32))
     if rows.count > rows.used:
-        for copy in range(copies):
-            out_ref[pl.ds(copy * rows.count + rows.used, rows.count - rows.used), :] = jnp.zeros(
-                (rows.count - rows.used, LANES), jnp.float32
-            )
+        block_ref[rows.used :, :] = jnp.zeros((rows.count - rows.used, LANES), jnp.float32)
+    block = block_ref[...]
+    for copy in range(copies):
+        out_ref[pl.ds(copy * rows.count, rows.count), :] = block
 
 
 SHRINK = 1.0 / 4.0
@@ -225,6 +224,7 @@
     tiles = index_ref.shape[0]
     block_copy = pltpu.make_async_copy(block_hbm, block_ref, sem_ref)
     block_copy.start()
+    live = live_ref[0, 0]
     holders = place()
     starts = [rows.coords[0], rows.coords[1], rows.coords[2], rows.charge]
     entry_rows = 6 * shell_rows
@@ -245,8 +245,6 @@
                 table_ref[c, at] = broadcast(slab_ref[pl.ds(c * shell_rows + part, 1), :] * factor)
                 at += 1
 
-    live = live_ref[0, 0]
-    down = lax.broadcasted_iota(jnp.int32, (SUBLANES, LANES), 0)
     for group in range(tiles // SUBLANES):
         at = pl.ds(group * SUBLANES, SUBLANES)
         index = index_ref[at, :]
@@ -256,12 +254,13 @@
         for k in range(entry_rows):
             here = chunk == atom_rows + k
             values = [jnp.where(here, take_lanes(table_ref[c, k], lanes), values[c]) for c in range(4)]
-        values[0] = jnp.where(down + group * SUBLANES < live, values[0], OUT_OF_REACH)
         for c in range(4):
             far_ref[c, at, :] = values[c]
 
     sum_ref[...] = jnp.zeros(sum_ref.shape, jnp.float32)
     block_copy.wait()
+    down = lax.broadcasted_iota(jnp.int32, (tiles, LANES), 0)
+    far_ref[0] = jnp.where(down < live, far_ref[0], OUT_OF_REACH)
 
     softening = 1.0 / cutoff_sq
 
@@ -396,7 +395,6 @@
     coords_out_ref,
     velocity_out_ref,
     push_ref,
-    far_push_ref,
     field_ref,
 ):
     atom_rows, shell_rows = rows.atom_rows, rows.shell_rows
@@ -460,16 +458,11 @@
             for c in range(3):
                 pushed = weight(at, c) * value
                 high = pushed.astype(jnp.bfloat16).astype(jnp.float32)
-                for row, part in ((c, high), (3 + c, pushed - high)):
-                    push_ref[at, pl.ds(row * domains, domains), :] = part
-                    if at >= bond_rows:
-                        for code in range(4):
-                            far_push_ref[at - bond_rows, pl.ds((code * SUBLANES + row) * domains, domains), :] = (
-                                jnp.where(sides[at - bond_rows] == code, part, 0.0)
-                            )
+                push_ref[at, pl.ds(c * domains, domains), :] = high
+                push_ref[at, pl.ds((3 + c) * domains, domains), :] = pushed - high
 
     def pushes_of(at, domain):
-        return push_ref[at, pl.ds(domain, SUBLANES, stride=domains), :].astype(jnp.bfloat16)
+        return push_ref[at, pl.ds(domain, SUBLANES, stride=domains), :]
 
     def product(pushes, domain, at):
         start = domain * rows.matrix + at
@@ -477,27 +470,31 @@
             start = pl.multiple_of(start, LANES)
         pushes = pushes[0] if len(pushes) == 1 else jnp.concatenate(pushes, axis=1)
         result = jnp.dot(
-            pushes, matrix_ref[pl.ds(start, pushes.shape[1]), :], preferred_element_type=jnp.float32
+            pushes.astype(jnp.bfloat16),
+            matrix_ref[pl.ds(start, pushes.shape[1]), :],
+            preferred_element_type=jnp.float32,
         )
         return [result[:, p * LANES : (p + 1) * LANES] for p in range(shell_rows)]
 
-    def inner_totals(domain):
-        pushes = [pushes_of(at, domain) for at in range(bond_rows + slot_rows)]
+    def inner_totals(pushes, domain):
         return product(pushes, domain, 0) + product(pushes[:bond_rows], domain, rows.shell_terms)
 
-    def far_totals(domain, first_row, count):
-        pushes = [
-            far_push_ref[p, pl.ds(first_row * domains + domain, count, stride=domains), :].astype(jnp.bfloat16)
-            for p in range(slot_rows)
-        ]
-        return product(pushes, domain, rows.far_at)
+    def far_totals(pushes, domain, codes):
+        masked = []
+        for part in range(slot_rows):
+            side = moves_ref[pl.ds(domain * rows.disp_count + rows.side + part, 1), :]
+            side = jnp.broadcast_to(side, (SUBLANES, LANES))
+            pushed = pushes[bond_rows + part]
+            masked.append(jnp.concatenate([jnp.where(side == code, pushed, 0.0) for code in codes], axis=0))
+        return product(masked, domain, rows.far_at)
 
     def spread(values):
         put_pushes(values)
         for domain in range(domains):
-            for part, total in enumerate(inner_totals(domain)):
+            pushes = [pushes_of(at, domain) for at in range(bond_rows + slot_rows)]
+            for part, total in enumerate(inner_totals(pushes, domain)):
                 field_ref[0, part, pl.ds(domain, SUBLANES, stride=domains), :] = total
-            for part, total in enumerate(far_totals(domain, 0, 4 * SUBLANES)):
+            for part, total in enumerate(far_totals(pushes, domain, range(4))):
                 for code, stride in enumerate(strides):
                     field_ref[1 + code, part, pl.ds((domain + stride) % domains, SUBLANES, stride=domains), :] = total[
                         code * SUBLANES : (code + 1) * SUBLANES, :
@@ -518,7 +515,6 @@
         for c in range(3)
     ]
     push_ref[...] = jnp.zeros(push_ref.shape, jnp.float32)
-    far_push_ref[...] = jnp.zeros(far_push_ref.shape, jnp.float32)
     residue = project(moves)
 
     def expand(_, carry):
@@ -529,10 +525,11 @@
 
     residue, summed = lax.fori_loop(0, ORDER, expand, (residue, residue))
     put_pushes(summed)
-    sums = inner_totals(me)
+    sums = inner_totals([pushes_of(at, me) for at in range(bond_rows + slot_rows)], me)
     for code, stride in enumerate(strides):
         owner = lax.rem(me + (-stride) % domains, domains)
-        for part, total in enumerate(far_totals(owner, code * SUBLANES, SUBLANES)):
+        pushes = [pushes_of(at, owner) for at in range(bond_rows + slot_rows)]
+        for part, total in enumerate(far_totals(pushes, owner, [code])):
             sums[part] = sums[part] + total
     for part in range(atom_rows):
         lanes = slice(part * LANES, (part + 1) * LANES)
@@ -604,7 +601,8 @@
         ),
         in_specs=hbm(len(sent)),
         out_specs=tuple(vmem(2)),
-        scratch_shapes=room_for(sent) + [pltpu.SemaphoreType.DMA((len(sent),))],
+        scratch_shapes=room_for(sent)
+        + [pltpu.SemaphoreType.DMA((len(sent),)), pltpu.VMEM((rows.count, LANES), f32)],
         compiler_params=params(4),
         name="pack",
     )(*in_hbm(sent))
@@ -687,7 +685,6 @@
         out_specs=tuple(vmem(2)),
         scratch_shapes=[
             pltpu.VMEM((constraint_rows, SUBLANES * domains, LANES), f32),
-            pltpu.VMEM((rows.slot_rows, 4 * SUBLANES * domains, LANES), f32),
             pltpu.VMEM((5, rows.atom_rows, SUBLANES * domains, LANES), f32),
         ],
         compiler_params=params(16),

time: 33 us -> 33 us (level)
  starting transfers between devices: 18.1 us -> 16.4 us
  Pallas kernels: 12 us -> 13.2 us
  waiting for transfers between devices: 0.55 us -> 1.04 us
    all_to_all x2, starting transfers between devices: 17.5 us -> 15.8 us  [from_slab(): lax.all_to_all(blocks, 'dom', 0, 0, axis_index_groups=[order], tiled=True)]
    pallas_call x1, Pallas kernels: 2.26 us -> 3.46 us  [shards(): pl.pallas_call(functools.partial(force_kernel, rows, copies, place), out_...]
    all_to_all x2, waiting for transfers between devices: 0.38 us -> 0.86 us  [from_slab(): lax.all_to_all(blocks, 'dom', 0, 0, axis_index_groups=[order], tiled=True)]
where the time goes in v2:
time: 33 us; the launch traced here: 32.6 us
  starting transfers between devices  16.4 us (50%)
  Pallas kernels  13.2 us (40%)
  between operations  1.97 us (6%)
  waiting for transfers between devices  1.04 us (3%)
    all_to_all x2, starting transfers between devices, from_slab(): lax.all_to_all(blocks, 'dom', 0, 0, axis_index_groups=[order], tiled=True)  15.8 us
    pallas_call x1, Pallas kernels, shards(): pl.pallas_call(functools.partial(solve_kernel, rows, domains, strides), o...  4.11 us
    pallas_call x1, Pallas kernels, shards(): pl.pallas_call(functools.partial(force_kernel, rows, copies, place), out_...  3.46 us
    pallas_call x1, Pallas kernels, shards(): pl.pallas_call(functools.partial(bond_kernel, rows, domains, strides), ou...  2.65 us
    pallas_call x1, Pallas kernels, shards(): pl.pallas_call(functools.partial(own_kernel, rows), out_shape=(jax.ShapeD...  1.54 us
    pallas_call x1, Pallas kernels, shards(): pl.pallas_call(functools.partial(pack_kernel, rows, copies), out_shape=(j...  1.44 us
    all_to_all x2, waiting for transfers between devices, from_slab(): lax.all_to_all(blocks, 'dom', 0, 0, axis_index_groups=[order], tiled=True)  0.86 us
  transfers between devices with their start and end apart: 4, of which 2 were waited for; matrix products, arithmetic and copies ran while one was open for 0% of the time, Pallas kernels for 13%

profile of v2, /device:TPU:0, one launch (start us, length us, event | category | flops | bytes accessed | tf_op | source)
XLA Modules:
  0.0 32.6 jit_solution(17803688081166257173)
XLA Ops:
  0.6 1.4 %pack.1 = (f32[192,128]{1,0:T(8,128)}, f32[8,128]{1,0:T(8,128)S(1)}) custom-call(f32[3,1,1,512]{3,2,1,0:T(1,128)} %coords_hbm.1, f32[1,1,512]{2,1,0:T(1,128)} %charge_hbm.1, f32[1,1,512]{2,1,0:T(1,128)} %mass_hbm.1, s32[2,1,1,256]{3,2,1,0:T(1,128)} %refs_3_.1, s32[2,1,1,128]{3,2,1,0:T(1,128)} %refs_4_.1), custom_call_target="tpu_custom_call" | custom-call | tf_op jit(solution)/shard_map/pack/pallas_call | solution.py:596
  2.1 9.3 %all-to-all-start = ((f32[8,24,128]{2,1,0:T(8,128)}), f32[8,24,128]{2,1,0:T(8,128)S(1)}, u32[]{:S(2)}, u32[]{:S(2)}) async-start(f32[8,24,128]{2,1,0:T(8,128)} %bitcast), calls=%async_computation | async-start | bytes 196608 | tf_op jit(solution)/shard_map/all_to_all | solution.py:33
  11.4 0.7 %collective-permute-start.1 = (f32[8,128]{1,0:T(8,128)S(1)}, f32[8,128]{1,0:T(8,128)S(1)}, u32[]{:S(2)}, u32[]{:S(2)}) collective-permute-start(f32[8,128]{1,0:T(8,128)S(1)} %get-tuple-element.11), channel_id=1, source_target_pairs={{0,24},{8,0},{16,8},{24,16},{1,25},{9,1},{17,9},{25,17},{2,26},{10... | collective-permute-start | bytes 12296 | tf_op jit(solution)/shard_map/ppermute | solution.py:23
  12.0 0.0 collective-permute-start
  13.3 1.5 %own.1 = (f32[4,512,128]{2,1,0:T(8,128)S(1)}, f32[4,64,128]{2,1,0:T(8,128)S(1)}, s32[64,128]{1,0:T(8,128)S(1)}, f32[17,128]{1,0:T(8,128)S(1)}) custom-call(f32[3,1,1,512]{3,2,1,0:T(1,128)} %coords_hbm.1, f32[1,1,512]{2,1,0:T(1,128)} %charge_hbm.1, f32[3,1,1,512]{3,2,1,0:T(1,128)} %velocity_hbm.1, f32[1,1,512]{2,1,0:T(1,128)} %mass_hbm.1, ...), custom_call_target="tpu_custom_call" | custom-call | flops 4194304 | bytes 1048576 | tf_op jit(solution)/shard_map/own/pallas_call | solution.py:611
  14.9 0.0 collective-permute-done.1.above_ref
  14.9 0.2 collective-permute-done.below_ref
  15.0 0.0 all-to-all-done
  15.0 3.5 %force.1 = f32[128,128]{1,0:T(8,128)} custom-call(s32[1,1]{1,0:T(1,128)S(6)} %copy.13.live_ref, s32[1,1]{1,0:T(1,128)S(6)} %copy.14.count_ref, s32[1,1,64]{2,1,0:T(1,128)} %block_hbm.1, f32[192,128]{1,0:T(8,128)S(1)} %bitcast.4, f32[8,128]{1,0:T(8,128)S(1)} %collective-permute-done.below_ref, f32[8,128]{1,0:T(8,128)S(1)} %collective-permute-done.1.above_ref, ...), custom_call_target="tpu_custom_call" | custom-call | flops 31457280 | bytes 98304 | tf_op jit(solution)/shard_map/force/pallas_call | solution.py:642
  18.5 6.5 %all-to-all-start.1 = ((f32[8,16,128]{2,1,0:T(8,128)}), f32[8,16,128]{2,1,0:T(8,128)S(1)}, u32[]{:S(2)}, u32[]{:S(2)}) async-start(f32[8,16,128]{2,1,0:T(8,128)} %bitcast.2), calls=%async_computation.1 | async-start | bytes 131072 | tf_op jit(solution)/shard_map/all_to_all | solution.py:33
  25.0 2.7 %bonds.1 = (f32[144,128]{1,0:T(8,128)S(1)}, bf16[6144,256]{1,0:T(8,128)(2,1)S(1)}) custom-call(f32[192,128]{1,0:T(8,128)S(1)} %bitcast.5), custom_call_target="tpu_custom_call" | custom-call | flops 12582912 | bytes 98304 | tf_op jit(solution)/shard_map/bonds/pallas_call | solution.py:663
  27.7 0.9 %all-to-all-done.1 = f32[8,16,128]{2,1,0:T(8,128)S(1)} async-done(((f32[8,16,128]{2,1,0:T(8,128)}), f32[8,16,128]{2,1,0:T(8,128)S(1)}, u32[]{:S(2)}, u32[]{:S(2)}) %all-to-all-start.1) | async-done | bytes 65568 | tf_op jit(solution)/shard_map/all_to_all | solution.py:33
  28.5 4.1 %solve.1 = (f32[3,1,1,512]{3,2,1,0:T(1,128)}, f32[3,1,1,512]{3,2,1,0:T(1,128)}) custom-call(f32[192,128]{1,0:T(8,128)S(1)} %bitcast.6, f32[128,128]{1,0:T(8,128)S(1)} %bitcast.7, f32[144,128]{1,0:T(8,128)S(1)} %get-tuple-element.16.weight_ref, bf16[6144,256]{1,0:T(8,128)(2,1)S(1)} %get-tuple-element.17.matrix_ref), custom_call_target="tpu_custom_call" | custom-call | tf_op jit(solution)/shard_map/solve/pallas_call | solution.py:678
Async XLA Ops:
  2.1 13.0 %all-to-all-start = ((f32[8,24,128]{2,1,0:T(8,128)}), f32[8,24,128]{2,1,0:T(8,128)S(1)}, u32[]{:S(2)}, u32[]{:S(2)}) async-start(f32[8,24,128]{2,1,0:T(8,128)} %bitcast), calls=%async_computation | async-start | bytes 196608 | tf_op jit(solution)/shard_map/all_to_all | solution.py:33
  11.4 3.5 %collective-permute-start.1 = (f32[8,128]{1,0:T(8,128)S(1)}, f32[8,128]{1,0:T(8,128)S(1)}, u32[]{:S(2)}, u32[]{:S(2)}) collective-permute-start(f32[8,128]{1,0:T(8,128)S(1)} %get-tuple-element.11), channel_id=1, source_target_pairs={{0,24},{8,0},{16,8},{24,16},{1,25},{9,1},{17,9},{25,17},{2,26},{10... | collective-permute-start | bytes 12296 | tf_op jit(solution)/shard_map/ppermute | solution.py:23
  12.0 3.0 %collective-permute-start = (f32[8,128]{1,0:T(8,128)S(1)}, f32[8,128]{1,0:T(8,128)S(1)}, u32[]{:S(2)}, u32[]{:S(2)}) collective-permute-start(f32[8,128]{1,0:T(8,128)S(1)} %get-tuple-element.11), channel_id=1, source_target_pairs={{0,8},{8,16},{16,24},{24,0},{1,9},{9,17},{17,25},{25,1},{2,10},{10... | collective-permute-start | bytes 12296 | tf_op jit(solution)/shard_map/ppermute | solution.py:23
  18.5 10.0 %all-to-all-start.1 = ((f32[8,16,128]{2,1,0:T(8,128)}), f32[8,16,128]{2,1,0:T(8,128)S(1)}, u32[]{:S(2)}, u32[]{:S(2)}) async-start(f32[8,16,128]{2,1,0:T(8,128)} %bitcast.2), calls=%async_computation.1 | async-start | bytes 131072 | tf_op jit(solution)/shard_map/all_to_all | solution.py:33

commit v3 on v2

--- a/solution.py
+++ b/solution.py
@@ -135,33 +135,66 @@
 
 SHRINK = 1.0 / 4.0
 OUT_OF_REACH = 1000.0
-TILES_STEP = 4
-PIECE = 32
+PAIRS_STEP = 2
+PIECE = 16
+
+
+def pair_up(block_ref, live, blocks, order_ref):
+    tiles = block_ref.shape[2]
+    shape = (tiles, LANES)
+    lane = lax.broadcasted_iota(jnp.int32, shape, 1)
+    tile = lax.broadcasted_iota(jnp.int32, shape, 0)
+    order_ref[...] = jnp.zeros(order_ref.shape, jnp.int32)
+    order_ref[0:1, :tiles] = block_ref[0]
+
+    def down(row):
+        row = jnp.broadcast_to(row, (SUBLANES, LANES))
+        start = lax.broadcasted_iota(jnp.int32, (SUBLANES, LANES), 0)
+        return jnp.concatenate([take_lanes(row, start + at) for at in range(0, tiles, SUBLANES)], axis=0)
+
+    across = jnp.where(lane[0:1] < live, order_ref[0:1, :], -1)
+    along = down(across)
+    rank = jnp.sum(jnp.where((along == across) & (tile < lane), 1, 0), axis=0, keepdims=True)
+    start = jnp.zeros((1, LANES), jnp.int32)
+    pairs = jnp.zeros((1, LANES), jnp.int32)
+    for block in range(blocks):
+        count = jnp.sum(jnp.where(across == block, 1.0, 0.0), axis=1, keepdims=True).astype(jnp.int32)
+        start = jnp.where(across == block, 2 * pairs, start)
+        pairs = pairs + ((count + 1) >> 1)
+    place = down(jnp.where(across < 0, -1, start + rank))
+    here = place == lane
+    order_ref[0:1, :] = tiles + jnp.sum(jnp.where(here, tile - tiles, 0), axis=0, keepdims=True)
+    order_ref[1:2, :] = jnp.sum(jnp.where(here, along, 0), axis=0, keepdims=True)
+    order_ref[2:3, :] = pairs
 
 
 def own_kernel(
     rows,
+    live_ref,
     coords_hbm,
     charge_hbm,
     velocity_hbm,
     mass_hbm,
     side_hbm,
+    block_hbm,
     atoms_hbm,
     own_ref,
     far_ref,
     index_ref,
     motion_ref,
+    order_ref,
     coords_ref,
     charge_ref,
     velocity_ref,
     mass_ref,
     side_ref,
+    block_ref,
     sem_ref,
 ):
     atom_rows = rows.atom_rows
     copies = fetched(
-        (coords_hbm, charge_hbm, atoms_hbm.at[0, 0], velocity_hbm, mass_hbm, side_hbm),
-        (coords_ref, charge_ref, index_ref, velocity_ref, mass_ref, side_ref),
+        (coords_hbm, charge_hbm, atoms_hbm.at[0, 0], velocity_hbm, mass_hbm, side_hbm, block_hbm),
+        (coords_ref, charge_ref, index_ref, velocity_ref, mass_ref, side_ref, block_ref),
         sem_ref,
     )
     down = lax.broadcasted_iota(jnp.int32, (SUBLANES, LANES), 0)
@@ -191,6 +224,7 @@
             far_ref[c, at, :] = pick(table[c], index)
     for copy in copies[3:]:
         copy.wait()
+    pair_up(block_ref, live_ref[0, 0], atom_rows * LANES // TILE, order_ref)
     fields = [velocity_ref[c, 0] for c in range(3)] + [mass_ref[0], side_ref[0].astype(jnp.float32)]
     at = 0
     for field in fields:
@@ -203,9 +237,8 @@
     rows,
     copies,
     place,
-    live_ref,
     count_ref,
-    block_hbm,
+    order_hbm,
     around_ref,
     below_ref,
     above_ref,
@@ -217,14 +250,13 @@
     table_ref,
     far_ref,
     sum_ref,
-    block_ref,
+    order_ref,
     sem_ref,
 ):
     atom_rows, shell_rows = rows.atom_rows, rows.shell_rows
     tiles = index_ref.shape[0]
-    block_copy = pltpu.make_async_copy(block_hbm, block_ref, sem_ref)
-    block_copy.start()
-    live = live_ref[0, 0]
+    order_copy = pltpu.make_async_copy(order_hbm, order_ref, sem_ref)
+    order_copy.start()
     holders = place()
     starts = [rows.coords[0], rows.coords[1], rows.coords[2], rows.charge]
     entry_rows = 6 * shell_rows
@@ -258,31 +290,39 @@
             far_ref[c, at, :] = values[c]
 
     sum_ref[...] = jnp.zeros(sum_ref.shape, jnp.float32)
-    block_copy.wait()
-    down = lax.broadcasted_iota(jnp.int32, (tiles, LANES), 0)
-    far_ref[0] = jnp.where(down < live, far_ref[0], OUT_OF_REACH)
+    far_ref[0, tiles:, :] = jnp.full((SUBLANES, LANES), OUT_OF_REACH, jnp.float32)
+    for c in range(1, 4):
+        far_ref[c, tiles:, :] = jnp.zeros((SUBLANES, LANES), jnp.float32)
+    order_copy.wait()
 
     softening = 1.0 / cutoff_sq
 
-    def add_tile(tile):
-        base = block_ref[0, 0, tile] * TILE
-        far = [jnp.broadcast_to(far_ref[c, pl.ds(tile, 1), :], (PIECE, LANES)) for c in range(4)]
+    def add_pair(pair):
+        base = order_ref[1, 2 * pair] * TILE
+        fars = [
+            [jnp.broadcast_to(far_ref[c, pl.ds(order_ref[0, 2 * pair + n], 1), :], (PIECE, LANES)) for c in range(4)]
+            for n in range(2)
+        ]
         for piece in range(TILE // PIECE):
             at = pl.ds(pl.multiple_of(base + piece * PIECE, PIECE), PIECE)
-            gap = [own_ref[c, at, :] - far[c] for c in range(3)]
-            square = gap[0] * gap[0] + gap[1] * gap[1] + gap[2] * gap[2]
-            inverse = pl.reciprocal(square + softening, approx=True)
-            weight = jnp.maximum(inverse - 1.0 / (1.0 + softening), 0.0)
-            strength = (inverse - own_ref[3, at, :] * far[3]) * (weight * weight)
+            own = [own_ref[c, at, :] for c in range(4)]
+            pushes = []
+            for far in fars:
+                gap = [own[c] - far[c] for c in range(3)]
+                square = gap[0] * gap[0] + gap[1] * gap[1] + gap[2] * gap[2]
+                inverse = pl.reciprocal(square + softening, approx=True)
+                weight = jnp.maximum(inverse - 1.0 / (1.0 + softening), 0.0)
+                strength = (inverse - own[3] * far[3]) * (weight * weight)
+                pushes.append([strength * gap[c] for c in range(3)])
             for c in range(3):
-                sum_ref[c, at, :] = sum_ref[c, at, :] + strength * gap[c]
-
-    def add_tiles(step, _):
-        for n in range(TILES_STEP):
-            add_tile(step * TILES_STEP + n)
+                sum_ref[c, at, :] = sum_ref[c, at, :] + (pushes[0][c] + pushes[1][c])
+
+    def add_pairs(step, _):
+        for n in range(PAIRS_STEP):
+            add_pair(step * PAIRS_STEP + n)
         return 0
 
-    lax.fori_loop(0, lax.div(live + TILES_STEP - 1, TILES_STEP), add_tiles, 0)
+    lax.fori_loop(0, lax.div(order_ref[2, 0] + PAIRS_STEP - 1, PAIRS_STEP), add_pairs, 0)
 
     scale = time_step * time_step * force_scale * 4.0 / 2048.0 * (1.0 + softening) ** 2
 
@@ -554,6 +594,10 @@
     return [pl.BlockSpec(memory_space=pltpu.HBM)] * count
 
 
+def any_space(count):
+    return [pl.BlockSpec(memory_space=pl.ANY)] * count
+
+
 def in_hbm(arrays):
     return [pltpu.with_memory_space_constraint(a, pltpu.HBM) for a in arrays]
 
@@ -607,22 +651,23 @@
         name="pack",
     )(*in_hbm(sent))
 
-    alone = (coords, charge, velocity, inv_mass, cross_side, tile_atoms)
-    own = pl.pallas_call(
+    alone = (coords, charge, velocity, inv_mass, cross_side, tile_block, tile_atoms)
+    *own, order = pl.pallas_call(
         functools.partial(own_kernel, rows),
         out_shape=(
             jax.ShapeDtypeStruct((4, atoms, LANES), f32),
             jax.ShapeDtypeStruct((4, tiles, TILE), f32),
             jax.ShapeDtypeStruct((tiles, TILE), jnp.int32),
             jax.ShapeDtypeStruct((4 * rows.atom_rows + rows.slot_rows, LANES), f32),
+            jax.ShapeDtypeStruct((SUBLANES, LANES), jnp.int32),
         ),
-        in_specs=hbm(len(alone)),
-        out_specs=tuple(vmem(4)),
-        scratch_shapes=room_for(alone[:5]) + [pltpu.SemaphoreType.DMA((len(alone),))],
+        in_specs=smem(1) + hbm(len(alone)),
+        out_specs=tuple(vmem(5)),
+        scratch_shapes=room_for(alone[:6]) + [pltpu.SemaphoreType.DMA((len(alone),))],
         compiler_params=params(4),
         cost_estimate=cost(64 * atoms * LANES, 16 * atoms * LANES),
         name="own",
-    )(*in_hbm(alone))
+    )(active_tile_count, *in_hbm(alone))
 
     below = passed_along(rim, "slab", 1)
     above = passed_along(rim, "slab", -1)
@@ -642,19 +687,19 @@
     moves = pl.pallas_call(
         functools.partial(force_kernel, rows, copies, place),
         out_shape=jax.ShapeDtypeStruct((copies * rows.disp_count, LANES), f32),
-        in_specs=smem(2) + hbm(1) + vmem(7),
+        in_specs=smem(1) + any_space(1) + vmem(7),
         out_specs=vmem(1)[0],
         scratch_shapes=[
             pltpu.VMEM((4, 6 * rows.shell_rows, SUBLANES, LANES), f32),
-            pltpu.VMEM((4, tiles, LANES), f32),
+            pltpu.VMEM((4, tiles + SUBLANES, LANES), f32),
             pltpu.VMEM((3, atoms, LANES), f32),
-            pltpu.SMEM(tile_block.shape, jnp.int32),
+            pltpu.SMEM(order.shape, jnp.int32),
             pltpu.SemaphoreType.DMA(()),
         ],
         compiler_params=params(8),
         cost_estimate=cost(30 * tiles * TILE * TILE, 4 * around.size),
         name="force",
-    )(active_tile_count, cross_count, *in_hbm([tile_block]), around, below, above, *own)
+    )(cross_count, order, around, below, above, *own)
 
     if not whole_slab:
         return by_exchange(rows, strides, around, moves, cross_count)

time: 33 us -> 33 us (level)
  Pallas kernels: 13.2 us -> 14.2 us
  starting transfers between devices: 16.4 us -> 15.9 us
  waiting for transfers between devices: 1.04 us -> 0.56 us
    pallas_call x1, Pallas kernels: 3.46 us -> 4.22 us  [shards(): pl.pallas_call(functools.partial(force_kernel, rows, copies, place), out_...]
    all_to_all x2, starting transfers between devices: 15.8 us -> 15.3 us  [from_slab(): lax.all_to_all(blocks, 'dom', 0, 0, axis_index_groups=[order], tiled=True)]
  transfers between devices with their start and end apart: 4 -> 4, of which waited for: 2 -> 1; matrix products, arithmetic and copies ran while one was open for 0% -> 0% of each run, Pallas kernels for 13% -> 14%
where the time goes in v3:
time: 33 us; the launch traced here: 32.7 us
  starting transfers between devices  15.9 us (48%)
  Pallas kernels  14.2 us (43%)
  between operations  1.99 us (6%)
  waiting for transfers between devices  0.56 us (2%)
    all_to_all x2, starting transfers between devices, from_slab(): lax.all_to_all(blocks, 'dom', 0, 0, axis_index_groups=[order], tiled=True)  15.3 us
    pallas_call x1, Pallas kernels, shards(): pl.pallas_call(functools.partial(force_kernel, rows, copies, place), out_...  4.22 us
    pallas_call x1, Pallas kernels, shards(): pl.pallas_call(functools.partial(solve_kernel, rows, domains, strides), o...  4.11 us
    pallas_call x1, Pallas kernels, shards(): pl.pallas_call(functools.partial(bond_kernel, rows, domains, strides), ou...  2.65 us
    pallas_call x1, Pallas kernels, shards(): pl.pallas_call(functools.partial(own_kernel, rows), out_shape=(jax.ShapeD...  1.8 us
    pallas_call x1, Pallas kernels, shards(): pl.pallas_call(functools.partial(pack_kernel, rows, copies), out_shape=(j...  1.44 us
  transfers between devices with their start and end apart: 4, of which 1 were waited for; matrix products, arithmetic and copies ran while one was open for 0% of the time, Pallas kernels for 14%

profile of v3, /device:TPU:0, one launch (start us, length us, event | category | flops | bytes accessed | tf_op | source)
XLA Modules:
  0.0 32.7 jit_solution(17432088915120695918)
XLA Ops:
  0.6 1.4 %pack.1 = (f32[192,128]{1,0:T(8,128)}, f32[8,128]{1,0:T(8,128)S(1)}) custom-call(f32[3,1,1,512]{3,2,1,0:T(1,128)} %coords_hbm.1, f32[1,1,512]{2,1,0:T(1,128)} %charge_hbm.1, f32[1,1,512]{2,1,0:T(1,128)} %mass_hbm.1, s32[2,1,1,256]{3,2,1,0:T(1,128)} %refs_3_.1, s32[2,1,1,128]{3,2,1,0:T(1,128)} %refs_4_.1), custom_call_target="tpu_custom_call" | custom-call | tf_op jit(solution)/shard_map/pack/pallas_call | solution.py:640
  2.1 9.3 %all-to-all-start = ((f32[8,24,128]{2,1,0:T(8,128)}), f32[8,24,128]{2,1,0:T(8,128)S(1)}, u32[]{:S(2)}, u32[]{:S(2)}) async-start(f32[8,24,128]{2,1,0:T(8,128)} %bitcast), calls=%async_computation | async-start | bytes 196608 | tf_op jit(solution)/shard_map/all_to_all | solution.py:33
  11.4 0.7 %collective-permute-start.1 = (f32[8,128]{1,0:T(8,128)S(1)}, f32[8,128]{1,0:T(8,128)S(1)}, u32[]{:S(2)}, u32[]{:S(2)}) collective-permute-start(f32[8,128]{1,0:T(8,128)S(1)} %get-tuple-element.13), channel_id=1, source_target_pairs={{0,24},{8,0},{16,8},{24,16},{1,25},{9,1},{17,9},{25,17},{2,26},{10... | collective-permute-start | bytes 12296 | tf_op jit(solution)/shard_map/ppermute | solution.py:23
  12.0 0.0 collective-permute-start
  13.3 1.8 %own.1 = (f32[4,512,128]{2,1,0:T(8,128)S(1)}, f32[4,64,128]{2,1,0:T(8,128)S(1)}, s32[64,128]{1,0:T(8,128)S(1)}, f32[17,128]{1,0:T(8,128)S(1)}, s32[8,128]{1,0:T(8,128)S(1)}) custom-call(s32[1,1]{1,0:T(1,128)S(6)} %copy.13.live_ref, f32[3,1,1,512]{3,2,1,0:T(1,128)} %coords_hbm.1, f32[1,1,512]{2,1,0:T(1,128)} %charge_hbm.1, f32[3,1,1,512]{3,2,1,0:T(1,128)} %velocity_hbm.1, ...), custom_call_target="tpu_custom_call" | custom-call | flops 4194304 | bytes 1048576 | tf_op jit(solution)/shard_map/own/pallas_call | solution.py:655
  15.1 0.0 collective-permute-done.1.above_ref
  15.1 0.0 collective-permute-done.below_ref
  15.1 0.0 all-to-all-done
  15.2 4.2 %force.1 = f32[128,128]{1,0:T(8,128)} custom-call(s32[1,1]{1,0:T(1,128)S(6)} %copy.14.count_ref, s32[8,128]{1,0:T(8,128)S(1)} %get-tuple-element.12.order_hbm, f32[192,128]{1,0:T(8,128)S(1)} %bitcast.4, f32[8,128]{1,0:T(8,128)S(1)} %collective-permute-done.below_ref, f32[8,128]{1,0:T(8,128)S(1)} %collective-permute-done.1.above_ref, ...), custom_call_target="tpu_custom_call" | custom-call | flops 31457280 | bytes 98304 | tf_op jit(solution)/shard_map/force/pallas_call | solution.py:687
  19.4 6.0 %all-to-all-start.1 = ((f32[8,16,128]{2,1,0:T(8,128)}), f32[8,16,128]{2,1,0:T(8,128)S(1)}, u32[]{:S(2)}, u32[]{:S(2)}) async-start(f32[8,16,128]{2,1,0:T(8,128)} %bitcast.2), calls=%async_computation.1 | async-start | bytes 131072 | tf_op jit(solution)/shard_map/all_to_all | solution.py:33
  25.4 2.7 %bonds.1 = (f32[144,128]{1,0:T(8,128)S(1)}, bf16[6144,256]{1,0:T(8,128)(2,1)S(1)}) custom-call(f32[192,128]{1,0:T(8,128)S(1)} %bitcast.5), custom_call_target="tpu_custom_call" | custom-call | flops 12582912 | bytes 98304 | tf_op jit(solution)/shard_map/bonds/pallas_call | solution.py:708
  28.0 0.6 %all-to-all-done.1 = f32[8,16,128]{2,1,0:T(8,128)S(1)} async-done(((f32[8,16,128]{2,1,0:T(8,128)}), f32[8,16,128]{2,1,0:T(8,128)S(1)}, u32[]{:S(2)}, u32[]{:S(2)}) %all-to-all-start.1) | async-done | bytes 65568 | tf_op jit(solution)/shard_map/all_to_all | solution.py:33
  28.6 4.1 %solve.1 = (f32[3,1,1,512]{3,2,1,0:T(1,128)}, f32[3,1,1,512]{3,2,1,0:T(1,128)}) custom-call(f32[192,128]{1,0:T(8,128)S(1)} %bitcast.6, f32[128,128]{1,0:T(8,128)S(1)} %bitcast.7, f32[144,128]{1,0:T(8,128)S(1)} %get-tuple-element.18.weight_ref, bf16[6144,256]{1,0:T(8,128)(2,1)S(1)} %get-tuple-element.19.matrix_ref), custom_call_target="tpu_custom_call" | custom-call | tf_op jit(solution)/shard_map/solve/pallas_call | solution.py:723
Async XLA Ops:
  2.1 13.1 %all-to-all-start = ((f32[8,24,128]{2,1,0:T(8,128)}), f32[8,24,128]{2,1,0:T(8,128)S(1)}, u32[]{:S(2)}, u32[]{:S(2)}) async-start(f32[8,24,128]{2,1,0:T(8,128)} %bitcast), calls=%async_computation | async-start | bytes 196608 | tf_op jit(solution)/shard_map/all_to_all | solution.py:33
  11.4 3.8 %collective-permute-start.1 = (f32[8,128]{1,0:T(8,128)S(1)}, f32[8,128]{1,0:T(8,128)S(1)}, u32[]{:S(2)}, u32[]{:S(2)}) collective-permute-start(f32[8,128]{1,0:T(8,128)S(1)} %get-tuple-element.13), channel_id=1, source_target_pairs={{0,24},{8,0},{16,8},{24,16},{1,25},{9,1},{17,9},{25,17},{2,26},{10... | collective-permute-start | bytes 12296 | tf_op jit(solution)/shard_map/ppermute | solution.py:23
  12.0 3.1 %collective-permute-start = (f32[8,128]{1,0:T(8,128)S(1)}, f32[8,128]{1,0:T(8,128)S(1)}, u32[]{:S(2)}, u32[]{:S(2)}) collective-permute-start(f32[8,128]{1,0:T(8,128)S(1)} %get-tuple-element.13), channel_id=1, source_target_pairs={{0,8},{8,16},{16,24},{24,0},{1,9},{9,17},{17,25},{25,1},{2,10},{10... | collective-permute-start | bytes 12296 | tf_op jit(solution)/shard_map/ppermute | solution.py:23
  19.4 9.2 %all-to-all-start.1 = ((f32[8,16,128]{2,1,0:T(8,128)}), f32[8,16,128]{2,1,0:T(8,128)S(1)}, u32[]{:S(2)}, u32[]{:S(2)}) async-start(f32[8,16,128]{2,1,0:T(8,128)} %bitcast.2), calls=%async_computation.1 | async-start | bytes 131072 | tf_op jit(solution)/shard_map/all_to_all | solution.py:33

commit v4 on v2

--- a/solution.py
+++ b/solution.py
@@ -271,7 +271,8 @@
             at = pl.ds(pl.multiple_of(base + piece * PIECE, PIECE), PIECE)
             gap = [own_ref[c, at, :] - far[c] for c in range(3)]
             square = gap[0] * gap[0] + gap[1] * gap[1] + gap[2] * gap[2]
-            inverse = pl.reciprocal(square + softening, approx=True)
+            root = lax.rsqrt(square + softening)
+            inverse = root * root
             weight = jnp.maximum(inverse - 1.0 / (1.0 + softening), 0.0)
             strength = (inverse - own_ref[3, at, :] * far[3]) * (weight * weight)
             for c in range(3):

time: 33 us -> 33.7 us (1.021)
  starting transfers between devices: 16.4 us -> 19.1 us
  Pallas kernels: 13.2 us -> 11.8 us
  waiting for transfers between devices: 1.04 us -> 0.55 us
    all_to_all x2, starting transfers between devices: 15.8 us -> 18.4 us  [from_slab(): lax.all_to_all(blocks, 'dom', 0, 0, axis_index_groups=[order], tiled=True)]
    pallas_call x1, Pallas kernels: 3.46 us -> 2.08 us  [shards(): pl.pallas_call(functools.partial(force_kernel, rows, copies, place), out_...]
    all_to_all x2, waiting for transfers between devices: 0.86 us -> 0.38 us  [from_slab(): lax.all_to_all(blocks, 'dom', 0, 0, axis_index_groups=[order], tiled=True)]
where the time goes in v4:
time: 33.7 us; the launch traced here: 33.4 us
  starting transfers between devices  19.1 us (57%)
  Pallas kernels  11.8 us (35%)
  between operations  1.97 us (6%)
  waiting for transfers between devices  0.55 us (2%)
    all_to_all x2, starting transfers between devices, from_slab(): lax.all_to_all(blocks, 'dom', 0, 0, axis_index_groups=[order], tiled=True)  18.4 us
    pallas_call x1, Pallas kernels, shards(): pl.pallas_call(functools.partial(solve_kernel, rows, domains, strides), o...  4.11 us
    pallas_call x1, Pallas kernels, shards(): pl.pallas_call(functools.partial(bond_kernel, rows, domains, strides), ou...  2.65 us
    pallas_call x1, Pallas kernels, shards(): pl.pallas_call(functools.partial(force_kernel, rows, copies, place), out_...  2.08 us
    pallas_call x1, Pallas kernels, shards(): pl.pallas_call(functools.partial(own_kernel, rows), out_shape=(jax.ShapeD...  1.54 us
    pallas_call x1, Pallas kernels, shards(): pl.pallas_call(functools.partial(pack_kernel, rows, copies), out_shape=(j...  1.44 us
  transfers between devices with their start and end apart: 4, of which 2 were waited for; matrix products, arithmetic and copies ran while one was open for 0% of the time, Pallas kernels for 13%

profile of v4, /device:TPU:0, one launch (start us, length us, event | category | flops | bytes accessed | tf_op | source)
XLA Modules:
  0.0 33.4 jit_solution(8414855485984890375)
XLA Ops:
  0.6 1.4 %pack.1 = (f32[192,128]{1,0:T(8,128)}, f32[8,128]{1,0:T(8,128)S(1)}) custom-call(f32[3,1,1,512]{3,2,1,0:T(1,128)} %coords_hbm.1, f32[1,1,512]{2,1,0:T(1,128)} %charge_hbm.1, f32[1,1,512]{2,1,0:T(1,128)} %mass_hbm.1, s32[2,1,1,256]{3,2,1,0:T(1,128)} %refs_3_.1, s32[2,1,1,128]{3,2,1,0:T(1,128)} %refs_4_.1), custom_call_target="tpu_custom_call" | custom-call | tf_op jit(solution)/shard_map/pack/pallas_call | solution.py:597
  2.1 9.3 %all-to-all-start = ((f32[8,24,128]{2,1,0:T(8,128)}), f32[8,24,128]{2,1,0:T(8,128)S(1)}, u32[]{:S(2)}, u32[]{:S(2)}) async-start(f32[8,24,128]{2,1,0:T(8,128)} %bitcast), calls=%async_computation | async-start | bytes 196608 | tf_op jit(solution)/shard_map/all_to_all | solution.py:33
  11.4 0.7 %collective-permute-start.1 = (f32[8,128]{1,0:T(8,128)S(1)}, f32[8,128]{1,0:T(8,128)S(1)}, u32[]{:S(2)}, u32[]{:S(2)}) collective-permute-start(f32[8,128]{1,0:T(8,128)S(1)} %get-tuple-element.11), channel_id=1, source_target_pairs={{0,24},{8,0},{16,8},{24,16},{1,25},{9,1},{17,9},{25,17},{2,26},{10... | collective-permute-start | bytes 12296 | tf_op jit(solution)/shard_map/ppermute | solution.py:23
  12.0 0.0 collective-permute-start
  13.3 1.5 %own.1 = (f32[4,512,128]{2,1,0:T(8,128)S(1)}, f32[4,64,128]{2,1,0:T(8,128)S(1)}, s32[64,128]{1,0:T(8,128)S(1)}, f32[17,128]{1,0:T(8,128)S(1)}) custom-call(f32[3,1,1,512]{3,2,1,0:T(1,128)} %coords_hbm.1, f32[1,1,512]{2,1,0:T(1,128)} %charge_hbm.1, f32[3,1,1,512]{3,2,1,0:T(1,128)} %velocity_hbm.1, f32[1,1,512]{2,1,0:T(1,128)} %mass_hbm.1, ...), custom_call_target="tpu_custom_call" | custom-call | flops 4194304 | bytes 1048576 | tf_op jit(solution)/shard_map/own/pallas_call | solution.py:612
  14.9 0.0 collective-permute-done.1.above_ref
  14.9 0.2 collective-permute-done.below_ref
  15.0 0.0 all-to-all-done
  15.0 2.1 %force.1 = f32[128,128]{1,0:T(8,128)} custom-call(s32[1,1]{1,0:T(1,128)S(6)} %copy.13.live_ref, s32[1,1]{1,0:T(1,128)S(6)} %copy.14.count_ref, s32[1,1,64]{2,1,0:T(1,128)} %block_hbm.1, f32[192,128]{1,0:T(8,128)S(1)} %bitcast.4, f32[8,128]{1,0:T(8,128)S(1)} %collective-permute-done.below_ref, f32[8,128]{1,0:T(8,128)S(1)} %collective-permute-done.1.above_ref, ...), custom_call_target="tpu_custom_call" | custom-call | flops 31457280 | bytes 98304 | tf_op jit(solution)/shard_map/force/pallas_call | solution.py:643
  17.1 9.1 %all-to-all-start.1 = ((f32[8,16,128]{2,1,0:T(8,128)}), f32[8,16,128]{2,1,0:T(8,128)S(1)}, u32[]{:S(2)}, u32[]{:S(2)}) async-start(f32[8,16,128]{2,1,0:T(8,128)} %bitcast.2), calls=%async_computation.1 | async-start | bytes 131072 | tf_op jit(solution)/shard_map/all_to_all | solution.py:33
  26.3 2.7 %bonds.1 = (f32[144,128]{1,0:T(8,128)S(1)}, bf16[6144,256]{1,0:T(8,128)(2,1)S(1)}) custom-call(f32[192,128]{1,0:T(8,128)S(1)} %bitcast.5), custom_call_target="tpu_custom_call" | custom-call | flops 12582912 | bytes 98304 | tf_op jit(solution)/shard_map/bonds/pallas_call | solution.py:664
  28.9 0.4 %all-to-all-done.1 = f32[8,16,128]{2,1,0:T(8,128)S(1)} async-done(((f32[8,16,128]{2,1,0:T(8,128)}), f32[8,16,128]{2,1,0:T(8,128)S(1)}, u32[]{:S(2)}, u32[]{:S(2)}) %all-to-all-start.1) | async-done | bytes 65568 | tf_op jit(solution)/shard_map/all_to_all | solution.py:33
  29.3 4.1 %solve.1 = (f32[3,1,1,512]{3,2,1,0:T(1,128)}, f32[3,1,1,512]{3,2,1,0:T(1,128)}) custom-call(f32[192,128]{1,0:T(8,128)S(1)} %bitcast.6, f32[128,128]{1,0:T(8,128)S(1)} %bitcast.7, f32[144,128]{1,0:T(8,128)S(1)} %get-tuple-element.16.weight_ref, bf16[6144,256]{1,0:T(8,128)(2,1)S(1)} %get-tuple-element.17.matrix_ref), custom_call_target="tpu_custom_call" | custom-call | tf_op jit(solution)/shard_map/solve/pallas_call | solution.py:679
Async XLA Ops:
  2.1 13.0 %all-to-all-start = ((f32[8,24,128]{2,1,0:T(8,128)}), f32[8,24,128]{2,1,0:T(8,128)S(1)}, u32[]{:S(2)}, u32[]{:S(2)}) async-start(f32[8,24,128]{2,1,0:T(8,128)} %bitcast), calls=%async_computation | async-start | bytes 196608 | tf_op jit(solution)/shard_map/all_to_all | solution.py:33
  11.4 3.5 %collective-permute-start.1 = (f32[8,128]{1,0:T(8,128)S(1)}, f32[8,128]{1,0:T(8,128)S(1)}, u32[]{:S(2)}, u32[]{:S(2)}) collective-permute-start(f32[8,128]{1,0:T(8,128)S(1)} %get-tuple-element.11), channel_id=1, source_target_pairs={{0,24},{8,0},{16,8},{24,16},{1,25},{9,1},{17,9},{25,17},{2,26},{10... | collective-permute-start | bytes 12296 | tf_op jit(solution)/shard_map/ppermute | solution.py:23
  12.0 3.0 %collective-permute-start = (f32[8,128]{1,0:T(8,128)S(1)}, f32[8,128]{1,0:T(8,128)S(1)}, u32[]{:S(2)}, u32[]{:S(2)}) collective-permute-start(f32[8,128]{1,0:T(8,128)S(1)} %get-tuple-element.11), channel_id=1, source_target_pairs={{0,8},{8,16},{16,24},{24,0},{1,9},{9,17},{17,25},{25,1},{2,10},{10... | collective-permute-start | bytes 12296 | tf_op jit(solution)/shard_map/ppermute | solution.py:23
  17.1 12.2 %all-to-all-start.1 = ((f32[8,16,128]{2,1,0:T(8,128)}), f32[8,16,128]{2,1,0:T(8,128)S(1)}, u32[]{:S(2)}, u32[]{:S(2)}) async-start(f32[8,16,128]{2,1,0:T(8,128)} %bitcast.2), calls=%async_computation.1 | async-start | bytes 131072 | tf_op jit(solution)/shard_map/all_to_all | solution.py:33

commit v5 on v2

--- a/solution.py
+++ b/solution.py
@@ -104,11 +104,12 @@
 
 
 def pack_kernel(rows, copies, *refs):
-    sources, (out_ref, rim_ref), targets, sem_ref = refs[:5], refs[5:7], refs[7:12], refs[12]
-    block_ref = refs[13]
-    for copy in fetched(sources, targets, sem_ref):
+    sources, (out_ref, rim_ref), kept, (bonds_ref, cross_ref, block_ref, sem_ref) = refs[:8], refs[8:10], refs[10:16], refs[16:]
+    coords_ref, charge_ref, mass_ref, velocity_ref, side_ref, atoms_ref = kept
+    targets = (coords_ref, charge_ref, mass_ref, bonds_ref, cross_ref, velocity_ref, side_ref, atoms_ref)
+    fetches = fetched(sources, targets, sem_ref)
+    for copy in fetches[:5]:
         copy.wait()
-    coords_ref, charge_ref, mass_ref, bonds_ref, cross_ref = targets
 
     def put(row, value):
         for part in range(value.shape[1] // LANES):
@@ -131,6 +132,8 @@
     block = block_ref[...]
     for copy in range(copies):
         out_ref[pl.ds(copy * rows.count, rows.count), :] = block
+    for copy in fetches[5:]:
+        copy.wait()
 
 
 SHRINK = 1.0 / 4.0
@@ -140,33 +143,10 @@
 
 
 def own_kernel(
-    rows,
-    coords_hbm,
-    charge_hbm,
-    velocity_hbm,
-    mass_hbm,
-    side_hbm,
-    atoms_hbm,
-    own_ref,
-    far_ref,
-    index_ref,
-    motion_ref,
-    coords_ref,
-    charge_ref,
-    velocity_ref,
-    mass_ref,
-    side_ref,
-    sem_ref,
+    rows, coords_ref, charge_ref, mass_ref, velocity_ref, side_ref, atoms_ref, own_ref, far_ref, motion_ref
 ):
     atom_rows = rows.atom_rows
-    copies = fetched(
-        (coords_hbm, charge_hbm, atoms_hbm.at[0, 0], velocity_hbm, mass_hbm, side_hbm),
-        (coords_ref, charge_ref, index_ref, velocity_ref, mass_ref, side_ref),
-        sem_ref,
-    )
     down = lax.broadcasted_iota(jnp.int32, (SUBLANES, LANES), 0)
-    copies[0].wait()
-    copies[1].wait()
 
     def lanes_of(part):
         return slice(part * LANES, (part + 1) * LANES)
@@ -183,14 +163,11 @@
             for c in range(4):
                 value = take_lanes(table[c][part], down + group * SUBLANES)
                 own_ref[c, pl.ds(at, SUBLANES), :] = value if c < 3 else value * 8.0
-    copies[2].wait()
-    for group in range(index_ref.shape[0] // SUBLANES):
+    for group in range(atoms_ref.shape[2] // SUBLANES):
         at = pl.ds(group * SUBLANES, SUBLANES)
-        index = index_ref[at, :]
+        index = atoms_ref[0, 0, at, :]
         for c in range(4):
             far_ref[c, at, :] = pick(table[c], index)
-    for copy in copies[3:]:
-        copy.wait()
     fields = [velocity_ref[c, 0] for c in range(3)] + [mass_ref[0], side_ref[0].astype(jnp.float32)]
     at = 0
     for field in fields:
@@ -221,7 +198,7 @@
     sem_ref,
 ):
     atom_rows, shell_rows = rows.atom_rows, rows.shell_rows
-    tiles = index_ref.shape[0]
+    tiles = index_ref.shape[2]
     block_copy = pltpu.make_async_copy(block_hbm, block_ref, sem_ref)
     block_copy.start()
     live = live_ref[0, 0]
@@ -247,7 +224,7 @@
 
     for group in range(tiles // SUBLANES):
         at = pl.ds(group * SUBLANES, SUBLANES)
-        index = index_ref[at, :]
+        index = index_ref[0, 0, at, :]
         lanes = index & (LANES - 1)
         chunk = index >> 7
         values = [near_ref[c, at, :] for c in range(4)]
@@ -593,36 +570,36 @@
     f32 = jnp.float32
 
     sent = (coords, charge, inv_mass, bond_atoms, cross_atoms)
-    packed, rim = pl.pallas_call(
+    alone = (velocity, cross_side, tile_atoms)
+    kept = sent[:3] + alone
+    packed, rim, *kept = pl.pallas_call(
         functools.partial(pack_kernel, rows, copies),
         out_shape=(
             jax.ShapeDtypeStruct((copies * rows.count, LANES), f32),
             jax.ShapeDtypeStruct((4 * rows.shell_rows, LANES), f32),
+            *(jax.ShapeDtypeStruct(a.shape, a.dtype) for a in kept),
         ),
-        in_specs=hbm(len(sent)),
-        out_specs=tuple(vmem(2)),
-        scratch_shapes=room_for(sent)
-        + [pltpu.SemaphoreType.DMA((len(sent),)), pltpu.VMEM((rows.count, LANES), f32)],
+        in_specs=hbm(len(sent + alone)),
+        out_specs=tuple(vmem(2 + len(kept))),
+        scratch_shapes=room_for(sent[3:])
+        + [pltpu.VMEM((rows.count, LANES), f32), pltpu.SemaphoreType.DMA((len(sent + alone),))],
         compiler_params=params(4),
         name="pack",
-    )(*in_hbm(sent))
-
-    alone = (coords, charge, velocity, inv_mass, cross_side, tile_atoms)
-    own = pl.pallas_call(
+    )(*in_hbm(sent + alone))
+
+    own, near, motion = pl.pallas_call(
         functools.partial(own_kernel, rows),
         out_shape=(
             jax.ShapeDtypeStruct((4, atoms, LANES), f32),
             jax.ShapeDtypeStruct((4, tiles, TILE), f32),
-            jax.ShapeDtypeStruct((tiles, TILE), jnp.int32),
             jax.ShapeDtypeStruct((4 * rows.atom_rows + rows.slot_rows, LANES), f32),
         ),
-        in_specs=hbm(len(alone)),
-        out_specs=tuple(vmem(4)),
-        scratch_shapes=room_for(alone[:5]) + [pltpu.SemaphoreType.DMA((len(alone),))],
+        in_specs=vmem(len(kept)),
+        out_specs=tuple(vmem(3)),
         compiler_params=params(4),
         cost_estimate=cost(64 * atoms * LANES, 16 * atoms * LANES),
         name="own",
-    )(*in_hbm(alone))
+    )(*kept)
 
     below = passed_along(rim, "slab", 1)
     above = passed_along(rim, "slab", -1)
@@ -654,7 +631,7 @@
         compiler_params=params(8),
         cost_estimate=cost(30 * tiles * TILE * TILE, 4 * around.size),
         name="force",
-    )(active_tile_count, cross_count, *in_hbm([tile_block]), around, below, above, *own)
+    )(active_tile_count, cross_count, *in_hbm([tile_block]), around, below, above, own, near, kept[-1], motion)
 
     if not whole_slab:
         return by_exchange(rows, strides, around, moves, cross_count)

time: 33 us -> 32.7 us (level); the launches traced: 32.6 us -> 32.8 us
  Pallas kernels: 13.2 us -> 10.9 us
  starting transfers between devices: 16.4 us -> 18.5 us
  waiting for transfers between devices: 1.04 us -> 1.37 us
    all_to_all x2, starting transfers between devices: 15.8 us -> 17.9 us  [from_slab(): lax.all_to_all(blocks, 'dom', 0, 0, axis_index_groups=[order], tiled=True)]
    pallas_call x1, Pallas kernels: 3.46 us -> 1.86 us  [shards(): pl.pallas_call(functools.partial(force_kernel, rows, copies, place), out_...]
    ppermute x2, waiting for transfers between devices: 0.17 us -> 1.02 us  [passed_along(): lax.ppermute(array, axis, [(i, (i + by) % length) for i in range(length)])]
    pallas_call x1, Pallas kernels: 1.54 us -> 0.7 us  [shards(): pl.pallas_call(functools.partial(own_kernel, rows), out_shape=(jax.ShapeD...]
    all_to_all x2, waiting for transfers between devices: 0.86 us -> 0.35 us  [from_slab(): lax.all_to_all(blocks, 'dom', 0, 0, axis_index_groups=[order], tiled=True)]
  transfers between devices with their start and end apart: 4 -> 4, of which waited for: 2 -> 2; matrix products, arithmetic and copies ran while one was open for 0% -> 0% of each run, Pallas kernels for 13% -> 10%
where the time goes in v5:
time: 32.7 us; the launch traced here: 32.8 us
  starting transfers between devices  18.5 us (57%)
  Pallas kernels  10.9 us (33%)
  between operations  1.97 us (6%)
  waiting for transfers between devices  1.37 us (4%)
    all_to_all x2, starting transfers between devices, from_slab(): lax.all_to_all(blocks, 'dom', 0, 0, axis_index_groups=[order], tiled=True)  17.9 us
    pallas_call x1, Pallas kernels, shards(): pl.pallas_call(functools.partial(solve_kernel, rows, domains, strides), o...  4.11 us
    pallas_call x1, Pallas kernels, shards(): pl.pallas_call(functools.partial(bond_kernel, rows, domains, strides), ou...  2.65 us
    pallas_call x1, Pallas kernels, shards(): pl.pallas_call(functools.partial(force_kernel, rows, copies, place), out_...  1.86 us
    pallas_call x1, Pallas kernels, shards(): pl.pallas_call(functools.partial(pack_kernel, rows, copies), out_shape=(j...  1.57 us
    ppermute x2, waiting for transfers between devices, passed_along(): lax.ppermute(array, axis, [(i, (i + by) % length) for i in range(length)])  1.02 us
    pallas_call x1, Pallas kernels, shards(): pl.pallas_call(functools.partial(own_kernel, rows), out_shape=(jax.ShapeD...  0.7 us
  transfers between devices with their start and end apart: 4, of which 2 were waited for; matrix products, arithmetic and copies ran while one was open for 0% of the time, Pallas kernels for 10%

profile of v5, /device:TPU:0, one launch (start us, length us, event | category | flops | bytes accessed | tf_op | source)
XLA Modules:
  0.0 32.8 jit_solution(2669114043973464323)
XLA Ops:
  0.6 1.6 %pack.1 = (f32[192,128]{1,0:T(8,128)}, f32[8,128]{1,0:T(8,128)S(1)}, f32[3,1,1,512]{3,2,1,0:T(1,128)S(1)}, f32[1,1,512]{2,1,0:T(1,128)S(1)}, f32[1,1,512]{2,1,0:...) custom-call(f32[3,1,1,512]{3,2,1,0:T(1,128)} %refs_0_.1, ...), custom_call_target="tpu_custom_call" | custom-call | tf_op jit(solution)/shard_map/pack/pallas_call | solution.py:575
  2.2 9.3 %all-to-all-start = ((f32[8,24,128]{2,1,0:T(8,128)}), f32[8,24,128]{2,1,0:T(8,128)S(1)}, u32[]{:S(2)}, u32[]{:S(2)}) async-start(f32[8,24,128]{2,1,0:T(8,128)} %bitcast), calls=%async_computation | async-start | bytes 196608 | tf_op jit(solution)/shard_map/all_to_all | solution.py:33
  11.5 0.7 %collective-permute-start.1 = (f32[8,128]{1,0:T(8,128)S(1)}, f32[8,128]{1,0:T(8,128)S(1)}, u32[]{:S(2)}, u32[]{:S(2)}) collective-permute-start(f32[8,128]{1,0:T(8,128)S(1)} %get-tuple-element.16), channel_id=1, source_target_pairs={{0,24},{8,0},{16,8},{24,16},{1,25},{9,1},{17,9},{25,17},{2,26},{10... | collective-permute-start | bytes 12296 | tf_op jit(solution)/shard_map/ppermute | solution.py:23
  12.1 0.0 collective-permute-start
  13.4 0.7 %own.1 = (f32[4,512,128]{2,1,0:T(8,128)S(1)}, f32[4,64,128]{2,1,0:T(8,128)S(1)}, f32[17,128]{1,0:T(8,128)S(1)}) custom-call(f32[3,1,1,512]{3,2,1,0:T(1,128)S(1)} %get-tuple-element.17.coords_ref, f32[1,1,512]{2,1,0:T(1,128)S(1)} %get-tuple-element.18.charge_ref, f32[1,1,512]{2,1,0:T(1,128)S(1)} %get-tuple-element.19.mass_ref, ...), custom_call_target="tpu_custom_call" | custom-call | flops 4194304 | bytes 1048576 | tf_op jit(solution)/shard_map/own/pallas_call | solution.py:590
  14.1 0.0 collective-permute-done.1.above_ref
  14.2 1.0 %collective-permute-done.below_ref = f32[8,128]{1,0:T(8,128)S(1)} collective-permute-done((f32[8,128]{1,0:T(8,128)S(1)}, f32[8,128]{1,0:T(8,128)S(1)}, u32[]{:S(2)}, u32[]{:S(2)}) %collective-permute-start) | collective-permute-done | bytes 4128 | tf_op jit(solution)/shard_map/ppermute | solution.py:23
  15.2 0.0 all-to-all-done
  15.2 1.9 %force.1 = f32[128,128]{1,0:T(8,128)} custom-call(s32[1,1]{1,0:T(1,128)S(6)} %copy.13.live_ref, s32[1,1]{1,0:T(1,128)S(6)} %copy.14.count_ref, s32[1,1,64]{2,1,0:T(1,128)} %block_hbm.1, f32[192,128]{1,0:T(8,128)S(1)} %bitcast.4, f32[8,128]{1,0:T(8,128)S(1)} %collective-permute-done.below_ref, f32[8,128]{1,0:T(8,128)S(1)} %collective-permute-done.1.above_ref, ...), custom_call_target="tpu_custom_call" | custom-call | flops 31457280 | bytes 98304 | tf_op jit(solution)/shard_map/force/pallas_call | solution.py:619
  17.0 8.6 %all-to-all-start.1 = ((f32[8,16,128]{2,1,0:T(8,128)}), f32[8,16,128]{2,1,0:T(8,128)S(1)}, u32[]{:S(2)}, u32[]{:S(2)}) async-start(f32[8,16,128]{2,1,0:T(8,128)} %bitcast.2), calls=%async_computation.1 | async-start | bytes 131072 | tf_op jit(solution)/shard_map/all_to_all | solution.py:33
  25.6 2.7 %bonds.1 = (f32[144,128]{1,0:T(8,128)S(1)}, bf16[6144,256]{1,0:T(8,128)(2,1)S(1)}) custom-call(f32[192,128]{1,0:T(8,128)S(1)} %bitcast.5), custom_call_target="tpu_custom_call" | custom-call | flops 12582912 | bytes 98304 | tf_op jit(solution)/shard_map/bonds/pallas_call | solution.py:640
  28.3 0.3 %all-to-all-done.1 = f32[8,16,128]{2,1,0:T(8,128)S(1)} async-done(((f32[8,16,128]{2,1,0:T(8,128)}), f32[8,16,128]{2,1,0:T(8,128)S(1)}, u32[]{:S(2)}, u32[]{:S(2)}) %all-to-all-start.1) | async-done | bytes 65568 | tf_op jit(solution)/shard_map/all_to_all | solution.py:33
  28.6 4.1 %solve.1 = (f32[3,1,1,512]{3,2,1,0:T(1,128)}, f32[3,1,1,512]{3,2,1,0:T(1,128)}) custom-call(f32[192,128]{1,0:T(8,128)S(1)} %bitcast.6, f32[128,128]{1,0:T(8,128)S(1)} %bitcast.7, f32[144,128]{1,0:T(8,128)S(1)} %get-tuple-element.26.weight_ref, bf16[6144,256]{1,0:T(8,128)(2,1)S(1)} %get-tuple-element.27.matrix_ref), custom_call_target="tpu_custom_call" | custom-call | tf_op jit(solution)/shard_map/solve/pallas_call | solution.py:655
Async XLA Ops:
  2.2 13.0 %all-to-all-start = ((f32[8,24,128]{2,1,0:T(8,128)}), f32[8,24,128]{2,1,0:T(8,128)S(1)}, u32[]{:S(2)}, u32[]{:S(2)}) async-start(f32[8,24,128]{2,1,0:T(8,128)} %bitcast), calls=%async_computation | async-start | bytes 196608 | tf_op jit(solution)/shard_map/all_to_all | solution.py:33
  11.5 2.7 %collective-permute-start.1 = (f32[8,128]{1,0:T(8,128)S(1)}, f32[8,128]{1,0:T(8,128)S(1)}, u32[]{:S(2)}, u32[]{:S(2)}) collective-permute-start(f32[8,128]{1,0:T(8,128)S(1)} %get-tuple-element.16), channel_id=1, source_target_pairs={{0,24},{8,0},{16,8},{24,16},{1,25},{9,1},{17,9},{25,17},{2,26},{10... | collective-permute-start | bytes 12296 | tf_op jit(solution)/shard_map/ppermute | solution.py:23
  12.1 3.0 %collective-permute-start = (f32[8,128]{1,0:T(8,128)S(1)}, f32[8,128]{1,0:T(8,128)S(1)}, u32[]{:S(2)}, u32[]{:S(2)}) collective-permute-start(f32[8,128]{1,0:T(8,128)S(1)} %get-tuple-element.16), channel_id=1, source_target_pairs={{0,8},{8,16},{16,24},{24,0},{1,9},{9,17},{17,25},{25,1},{2,10},{10... | collective-permute-start | bytes 12296 | tf_op jit(solution)/shard_map/ppermute | solution.py:23
  17.0 11.6 %all-to-all-start.1 = ((f32[8,16,128]{2,1,0:T(8,128)}), f32[8,16,128]{2,1,0:T(8,128)S(1)}, u32[]{:S(2)}, u32[]{:S(2)}) async-start(f32[8,16,128]{2,1,0:T(8,128)} %bitcast.2), calls=%async_computation.1 | async-start | bytes 131072 | tf_op jit(solution)/shard_map/all_to_all | solution.py:33

commit v6 on v2

--- a/solution.py
+++ b/solution.py
@@ -245,8 +245,8 @@
                 table_ref[c, at] = broadcast(slab_ref[pl.ds(c * shell_rows + part, 1), :] * factor)
                 at += 1
 
-    for group in range(tiles // SUBLANES):
-        at = pl.ds(group * SUBLANES, SUBLANES)
+    def gather(group):
+        at = pl.ds(pl.multiple_of(group * SUBLANES, SUBLANES), SUBLANES)
         index = index_ref[at, :]
         lanes = index & (LANES - 1)
         chunk = index >> 7
@@ -256,6 +256,13 @@
             values = [jnp.where(here, take_lanes(table_ref[c, k], lanes), values[c]) for c in range(4)]
         for c in range(4):
             far_ref[c, at, :] = values[c]
+
+    def gather_groups(step, _):
+        for n in range(2):
+            gather(step * 2 + n)
+        return 0
+
+    lax.fori_loop(0, tiles // SUBLANES // 2, gather_groups, 0)
 
     sum_ref[...] = jnp.zeros(sum_ref.shape, jnp.float32)
     block_copy.wait()

time: 33 us -> 33.6 us (1.018)
  starting transfers between devices: 16.4 us -> 17.7 us
  waiting for transfers between devices: 1.04 us -> 0.55 us
    all_to_all x2, starting transfers between devices: 15.8 us -> 17.1 us  [from_slab(): lax.all_to_all(blocks, 'dom', 0, 0, axis_index_groups=[order], tiled=True)]
    all_to_all x2, waiting for transfers between devices: 0.86 us -> 0.38 us  [from_slab(): lax.all_to_all(blocks, 'dom', 0, 0, axis_index_groups=[order], tiled=True)]
where the time goes in v6:
time: 33.6 us; the launch traced here: 33.3 us
  starting transfers between devices  17.7 us (53%)
  Pallas kernels  13.1 us (39%)
  between operations  1.97 us (6%)
  waiting for transfers between devices  0.55 us (2%)
    all_to_all x2, starting transfers between devices, from_slab(): lax.all_to_all(blocks, 'dom', 0, 0, axis_index_groups=[order], tiled=True)  17.1 us
    pallas_call x1, Pallas kernels, shards(): pl.pallas_call(functools.partial(solve_kernel, rows, domains, strides), o...  4.11 us
    pallas_call x1, Pallas kernels, shards(): pl.pallas_call(functools.partial(force_kernel, rows, copies, place), out_...  3.34 us
    pallas_call x1, Pallas kernels, shards(): pl.pallas_call(functools.partial(bond_kernel, rows, domains, strides), ou...  2.65 us
    pallas_call x1, Pallas kernels, shards(): pl.pallas_call(functools.partial(own_kernel, rows), out_shape=(jax.ShapeD...  1.54 us
    pallas_call x1, Pallas kernels, shards(): pl.pallas_call(functools.partial(pack_kernel, rows, copies), out_shape=(j...  1.44 us
  transfers between devices with their start and end apart: 4, of which 2 were waited for; matrix products, arithmetic and copies ran while one was open for 0% of the time, Pallas kernels for 13%

profile of v6, /device:TPU:0, one launch (start us, length us, event | category | flops | bytes accessed | tf_op | source)
XLA Modules:
  0.0 33.3 jit_solution(3989740901102610301)
XLA Ops:
  0.6 1.4 %pack.1 = (f32[192,128]{1,0:T(8,128)}, f32[8,128]{1,0:T(8,128)S(1)}) custom-call(f32[3,1,1,512]{3,2,1,0:T(1,128)} %coords_hbm.1, f32[1,1,512]{2,1,0:T(1,128)} %charge_hbm.1, f32[1,1,512]{2,1,0:T(1,128)} %mass_hbm.1, s32[2,1,1,256]{3,2,1,0:T(1,128)} %refs_3_.1, s32[2,1,1,128]{3,2,1,0:T(1,128)} %refs_4_.1), custom_call_target="tpu_custom_call" | custom-call | tf_op jit(solution)/shard_map/pack/pallas_call | solution.py:603
  2.1 9.3 %all-to-all-start = ((f32[8,24,128]{2,1,0:T(8,128)}), f32[8,24,128]{2,1,0:T(8,128)S(1)}, u32[]{:S(2)}, u32[]{:S(2)}) async-start(f32[8,24,128]{2,1,0:T(8,128)} %bitcast), calls=%async_computation | async-start | bytes 196608 | tf_op jit(solution)/shard_map/all_to_all | solution.py:33
  11.4 0.7 %collective-permute-start.1 = (f32[8,128]{1,0:T(8,128)S(1)}, f32[8,128]{1,0:T(8,128)S(1)}, u32[]{:S(2)}, u32[]{:S(2)}) collective-permute-start(f32[8,128]{1,0:T(8,128)S(1)} %get-tuple-element.11), channel_id=1, source_target_pairs={{0,24},{8,0},{16,8},{24,16},{1,25},{9,1},{17,9},{25,17},{2,26},{10... | collective-permute-start | bytes 12296 | tf_op jit(solution)/shard_map/ppermute | solution.py:23
  12.0 0.0 collective-permute-start
  13.3 1.5 %own.1 = (f32[4,512,128]{2,1,0:T(8,128)S(1)}, f32[4,64,128]{2,1,0:T(8,128)S(1)}, s32[64,128]{1,0:T(8,128)S(1)}, f32[17,128]{1,0:T(8,128)S(1)}) custom-call(f32[3,1,1,512]{3,2,1,0:T(1,128)} %coords_hbm.1, f32[1,1,512]{2,1,0:T(1,128)} %charge_hbm.1, f32[3,1,1,512]{3,2,1,0:T(1,128)} %velocity_hbm.1, f32[1,1,512]{2,1,0:T(1,128)} %mass_hbm.1, ...), custom_call_target="tpu_custom_call" | custom-call | flops 4194304 | bytes 1048576 | tf_op jit(solution)/shard_map/own/pallas_call | solution.py:618
  14.9 0.0 collective-permute-done.1.above_ref
  14.9 0.2 collective-permute-done.below_ref
  15.0 0.0 all-to-all-done
  15.0 3.3 %force.1 = f32[128,128]{1,0:T(8,128)} custom-call(s32[1,1]{1,0:T(1,128)S(6)} %copy.13.live_ref, s32[1,1]{1,0:T(1,128)S(6)} %copy.14.count_ref, s32[1,1,64]{2,1,0:T(1,128)} %block_hbm.1, f32[192,128]{1,0:T(8,128)S(1)} %bitcast.4, f32[8,128]{1,0:T(8,128)S(1)} %collective-permute-done.below_ref, f32[8,128]{1,0:T(8,128)S(1)} %collective-permute-done.1.above_ref, ...), custom_call_target="tpu_custom_call" | custom-call | flops 31457280 | bytes 98304 | tf_op jit(solution)/shard_map/force/pallas_call | solution.py:649
  18.4 7.8 %all-to-all-start.1 = ((f32[8,16,128]{2,1,0:T(8,128)}), f32[8,16,128]{2,1,0:T(8,128)S(1)}, u32[]{:S(2)}, u32[]{:S(2)}) async-start(f32[8,16,128]{2,1,0:T(8,128)} %bitcast.2), calls=%async_computation.1 | async-start | bytes 131072 | tf_op jit(solution)/shard_map/all_to_all | solution.py:33
  26.2 2.7 %bonds.1 = (f32[144,128]{1,0:T(8,128)S(1)}, bf16[6144,256]{1,0:T(8,128)(2,1)S(1)}) custom-call(f32[192,128]{1,0:T(8,128)S(1)} %bitcast.5), custom_call_target="tpu_custom_call" | custom-call | flops 12582912 | bytes 98304 | tf_op jit(solution)/shard_map/bonds/pallas_call | solution.py:670
  28.8 0.4 %all-to-all-done.1 = f32[8,16,128]{2,1,0:T(8,128)S(1)} async-done(((f32[8,16,128]{2,1,0:T(8,128)}), f32[8,16,128]{2,1,0:T(8,128)S(1)}, u32[]{:S(2)}, u32[]{:S(2)}) %all-to-all-start.1) | async-done | bytes 65568 | tf_op jit(solution)/shard_map/all_to_all | solution.py:33
  29.2 4.1 %solve.1 = (f32[3,1,1,512]{3,2,1,0:T(1,128)}, f32[3,1,1,512]{3,2,1,0:T(1,128)}) custom-call(f32[192,128]{1,0:T(8,128)S(1)} %bitcast.6, f32[128,128]{1,0:T(8,128)S(1)} %bitcast.7, f32[144,128]{1,0:T(8,128)S(1)} %get-tuple-element.16.weight_ref, bf16[6144,256]{1,0:T(8,128)(2,1)S(1)} %get-tuple-element.17.matrix_ref), custom_call_target="tpu_custom_call" | custom-call | tf_op jit(solution)/shard_map/solve/pallas_call | solution.py:685
Async XLA Ops:
  2.1 13.0 %all-to-all-start = ((f32[8,24,128]{2,1,0:T(8,128)}), f32[8,24,128]{2,1,0:T(8,128)S(1)}, u32[]{:S(2)}, u32[]{:S(2)}) async-start(f32[8,24,128]{2,1,0:T(8,128)} %bitcast), calls=%async_computation | async-start | bytes 196608 | tf_op jit(solution)/shard_map/all_to_all | solution.py:33
  11.4 3.5 %collective-permute-start.1 = (f32[8,128]{1,0:T(8,128)S(1)}, f32[8,128]{1,0:T(8,128)S(1)}, u32[]{:S(2)}, u32[]{:S(2)}) collective-permute-start(f32[8,128]{1,0:T(8,128)S(1)} %get-tuple-element.11), channel_id=1, source_target_pairs={{0,24},{8,0},{16,8},{24,16},{1,25},{9,1},{17,9},{25,17},{2,26},{10... | collective-permute-start | bytes 12296 | tf_op jit(solution)/shard_map/ppermute | solution.py:23
  12.0 3.0 %collective-permute-start = (f32[8,128]{1,0:T(8,128)S(1)}, f32[8,128]{1,0:T(8,128)S(1)}, u32[]{:S(2)}, u32[]{:S(2)}) collective-permute-start(f32[8,128]{1,0:T(8,128)S(1)} %get-tuple-element.11), channel_id=1, source_target_pairs={{0,8},{8,16},{16,24},{24,0},{1,9},{9,17},{17,25},{25,1},{2,10},{10... | collective-permute-start | bytes 12296 | tf_op jit(solution)/shard_map/ppermute | solution.py:23
  18.4 10.8 %all-to-all-start.1 = ((f32[8,16,128]{2,1,0:T(8,128)}), f32[8,16,128]{2,1,0:T(8,128)S(1)}, u32[]{:S(2)}, u32[]{:S(2)}) async-start(f32[8,16,128]{2,1,0:T(8,128)} %bitcast.2), calls=%async_computation.1 | async-start | bytes 131072 | tf_op jit(solution)/shard_map/all_to_all | solution.py:33

commit v7 on v2

--- a/solution.py
+++ b/solution.py
@@ -523,7 +523,9 @@
         residue = [now - step for now, step in zip(residue, change)]
         return residue, [a + b for a, b in zip(summed, residue)]
 
-    residue, summed = lax.fori_loop(0, ORDER, expand, (residue, residue))
+    summed = residue
+    for step in range(ORDER):
+        residue, summed = expand(step, (residue, summed))
     put_pushes(summed)
     sums = inner_totals([pushes_of(at, me) for at in range(bond_rows + slot_rows)], me)
     for code, stride in enumerate(strides):

time: 33 us -> 33.2 us (level)
  Pallas kernels: 13.2 us -> 13.7 us
  starting transfers between devices: 16.4 us -> 15.9 us
    pallas_call x1, Pallas kernels: 3.46 us -> 4.06 us  [shards(): pl.pallas_call(functools.partial(force_kernel, rows, copies, place), out_...]
    all_to_all x2, starting transfers between devices: 15.8 us -> 15.3 us  [from_slab(): lax.all_to_all(blocks, 'dom', 0, 0, axis_index_groups=[order], tiled=True)]
where the time goes in v7:
time: 33.2 us; the launch traced here: 32.8 us
  starting transfers between devices  15.9 us (48%)
  Pallas kernels  13.7 us (41%)
  between operations  1.97 us (6%)
  waiting for transfers between devices  1.19 us (4%)
    all_to_all x2, starting transfers between devices, from_slab(): lax.all_to_all(blocks, 'dom', 0, 0, axis_index_groups=[order], tiled=True)  15.3 us
    pallas_call x1, Pallas kernels, shards(): pl.pallas_call(functools.partial(force_kernel, rows, copies, place), out_...  4.06 us
    pallas_call x1, Pallas kernels, shards(): pl.pallas_call(functools.partial(solve_kernel, rows, domains, strides), o...  4.02 us
    pallas_call x1, Pallas kernels, shards(): pl.pallas_call(functools.partial(bond_kernel, rows, domains, strides), ou...  2.65 us
    pallas_call x1, Pallas kernels, shards(): pl.pallas_call(functools.partial(own_kernel, rows), out_shape=(jax.ShapeD...  1.54 us
    pallas_call x1, Pallas kernels, shards(): pl.pallas_call(functools.partial(pack_kernel, rows, copies), out_shape=(j...  1.44 us
    all_to_all x2, waiting for transfers between devices, from_slab(): lax.all_to_all(blocks, 'dom', 0, 0, axis_index_groups=[order], tiled=True)  1.02 us
  transfers between devices with their start and end apart: 4, of which 2 were waited for; matrix products, arithmetic and copies ran while one was open for 0% of the time, Pallas kernels for 13%

profile of v7, /device:TPU:0, one launch (start us, length us, event | category | flops | bytes accessed | tf_op | source)
XLA Modules:
  0.0 32.8 jit_solution(15245227493953599642)
XLA Ops:
  0.6 1.4 %pack.1 = (f32[192,128]{1,0:T(8,128)}, f32[8,128]{1,0:T(8,128)S(1)}) custom-call(f32[3,1,1,512]{3,2,1,0:T(1,128)} %coords_hbm.1, f32[1,1,512]{2,1,0:T(1,128)} %charge_hbm.1, f32[1,1,512]{2,1,0:T(1,128)} %mass_hbm.1, s32[2,1,1,256]{3,2,1,0:T(1,128)} %refs_3_.1, s32[2,1,1,128]{3,2,1,0:T(1,128)} %refs_4_.1), custom_call_target="tpu_custom_call" | custom-call | tf_op jit(solution)/shard_map/pack/pallas_call | solution.py:598
  2.1 9.3 %all-to-all-start = ((f32[8,24,128]{2,1,0:T(8,128)}), f32[8,24,128]{2,1,0:T(8,128)S(1)}, u32[]{:S(2)}, u32[]{:S(2)}) async-start(f32[8,24,128]{2,1,0:T(8,128)} %bitcast), calls=%async_computation | async-start | bytes 196608 | tf_op jit(solution)/shard_map/all_to_all | solution.py:33
  11.4 0.7 %collective-permute-start.1 = (f32[8,128]{1,0:T(8,128)S(1)}, f32[8,128]{1,0:T(8,128)S(1)}, u32[]{:S(2)}, u32[]{:S(2)}) collective-permute-start(f32[8,128]{1,0:T(8,128)S(1)} %get-tuple-element.11), channel_id=1, source_target_pairs={{0,24},{8,0},{16,8},{24,16},{1,25},{9,1},{17,9},{25,17},{2,26},{10... | collective-permute-start | bytes 12296 | tf_op jit(solution)/shard_map/ppermute | solution.py:23
  12.0 0.0 collective-permute-start
  13.3 1.5 %own.1 = (f32[4,512,128]{2,1,0:T(8,128)S(1)}, f32[4,64,128]{2,1,0:T(8,128)S(1)}, s32[64,128]{1,0:T(8,128)S(1)}, f32[17,128]{1,0:T(8,128)S(1)}) custom-call(f32[3,1,1,512]{3,2,1,0:T(1,128)} %coords_hbm.1, f32[1,1,512]{2,1,0:T(1,128)} %charge_hbm.1, f32[3,1,1,512]{3,2,1,0:T(1,128)} %velocity_hbm.1, f32[1,1,512]{2,1,0:T(1,128)} %mass_hbm.1, ...), custom_call_target="tpu_custom_call" | custom-call | flops 4194304 | bytes 1048576 | tf_op jit(solution)/shard_map/own/pallas_call | solution.py:613
  14.9 0.0 collective-permute-done.1.above_ref
  14.9 0.2 collective-permute-done.below_ref
  15.0 0.0 all-to-all-done
  15.0 4.1 %force.1 = f32[128,128]{1,0:T(8,128)} custom-call(s32[1,1]{1,0:T(1,128)S(6)} %copy.13.live_ref, s32[1,1]{1,0:T(1,128)S(6)} %copy.14.count_ref, s32[1,1,64]{2,1,0:T(1,128)} %block_hbm.1, f32[192,128]{1,0:T(8,128)S(1)} %bitcast.4, f32[8,128]{1,0:T(8,128)S(1)} %collective-permute-done.below_ref, f32[8,128]{1,0:T(8,128)S(1)} %collective-permute-done.1.above_ref, ...), custom_call_target="tpu_custom_call" | custom-call | flops 31457280 | bytes 98304 | tf_op jit(solution)/shard_map/force/pallas_call | solution.py:644
  19.1 6.0 %all-to-all-start.1 = ((f32[8,16,128]{2,1,0:T(8,128)}), f32[8,16,128]{2,1,0:T(8,128)S(1)}, u32[]{:S(2)}, u32[]{:S(2)}) async-start(f32[8,16,128]{2,1,0:T(8,128)} %bitcast.2), calls=%async_computation.1 | async-start | bytes 131072 | tf_op jit(solution)/shard_map/all_to_all | solution.py:33
  25.1 2.7 %bonds.1 = (f32[144,128]{1,0:T(8,128)S(1)}, bf16[6144,256]{1,0:T(8,128)(2,1)S(1)}) custom-call(f32[192,128]{1,0:T(8,128)S(1)} %bitcast.5), custom_call_target="tpu_custom_call" | custom-call | flops 12582912 | bytes 98304 | tf_op jit(solution)/shard_map/bonds/pallas_call | solution.py:665
  27.8 1.0 %all-to-all-done.1 = f32[8,16,128]{2,1,0:T(8,128)S(1)} async-done(((f32[8,16,128]{2,1,0:T(8,128)}), f32[8,16,128]{2,1,0:T(8,128)S(1)}, u32[]{:S(2)}, u32[]{:S(2)}) %all-to-all-start.1) | async-done | bytes 65568 | tf_op jit(solution)/shard_map/all_to_all | solution.py:33
  28.8 4.0 %solve.1 = (f32[3,1,1,512]{3,2,1,0:T(1,128)}, f32[3,1,1,512]{3,2,1,0:T(1,128)}) custom-call(f32[192,128]{1,0:T(8,128)S(1)} %bitcast.6, f32[128,128]{1,0:T(8,128)S(1)} %bitcast.7, f32[144,128]{1,0:T(8,128)S(1)} %get-tuple-element.16.weight_ref, bf16[6144,256]{1,0:T(8,128)(2,1)S(1)} %get-tuple-element.17.matrix_ref), custom_call_target="tpu_custom_call" | custom-call | tf_op jit(solution)/shard_map/solve/pallas_call | solution.py:680
Async XLA Ops:
  2.1 13.0 %all-to-all-start = ((f32[8,24,128]{2,1,0:T(8,128)}), f32[8,24,128]{2,1,0:T(8,128)S(1)}, u32[]{:S(2)}, u32[]{:S(2)}) async-start(f32[8,24,128]{2,1,0:T(8,128)} %bitcast), calls=%async_computation | async-start | bytes 196608 | tf_op jit(solution)/shard_map/all_to_all | solution.py:33
  11.4 3.5 %collective-permute-start.1 = (f32[8,128]{1,0:T(8,128)S(1)}, f32[8,128]{1,0:T(8,128)S(1)}, u32[]{:S(2)}, u32[]{:S(2)}) collective-permute-start(f32[8,128]{1,0:T(8,128)S(1)} %get-tuple-element.11), channel_id=1, source_target_pairs={{0,24},{8,0},{16,8},{24,16},{1,25},{9,1},{17,9},{25,17},{2,26},{10... | collective-permute-start | bytes 12296 | tf_op jit(solution)/shard_map/ppermute | solution.py:23
  12.0 3.0 %collective-permute-start = (f32[8,128]{1,0:T(8,128)S(1)}, f32[8,128]{1,0:T(8,128)S(1)}, u32[]{:S(2)}, u32[]{:S(2)}) collective-permute-start(f32[8,128]{1,0:T(8,128)S(1)} %get-tuple-element.11), channel_id=1, source_target_pairs={{0,8},{8,16},{16,24},{24,0},{1,9},{9,17},{17,25},{25,1},{2,10},{10... | collective-permute-start | bytes 12296 | tf_op jit(solution)/shard_map/ppermute | solution.py:23
  19.1 9.7 %all-to-all-start.1 = ((f32[8,16,128]{2,1,0:T(8,128)}), f32[8,16,128]{2,1,0:T(8,128)S(1)}, u32[]{:S(2)}, u32[]{:S(2)}) async-start(f32[8,16,128]{2,1,0:T(8,128)} %bitcast.2), calls=%async_computation.1 | async-start | bytes 131072 | tf_op jit(solution)/shard_map/all_to_all | solution.py:33

commit v8 on v7

--- a/solution.py
+++ b/solution.py
@@ -686,7 +686,7 @@
         in_specs=vmem(4),
         out_specs=tuple(vmem(2)),
         scratch_shapes=[
-            pltpu.VMEM((constraint_rows, SUBLANES * domains, LANES), f32),
+            pltpu.VMEM((constraint_rows, SUBLANES * domains + SUBLANES, LANES), f32),
             pltpu.VMEM((5, rows.atom_rows, SUBLANES * domains, LANES), f32),
         ],
         compiler_params=params(16),

time: 33.2 us -> 33.1 us (level)
  starting transfers between devices: 15.9 us -> 18.5 us
  Pallas kernels: 13.7 us -> 11.9 us
  waiting for transfers between devices: 1.19 us -> 0.55 us
    all_to_all x2, starting transfers between devices: 15.3 us -> 17.9 us  [from_slab(): lax.all_to_all(blocks, 'dom', 0, 0, axis_index_groups=[order], tiled=True)]
    pallas_call x1, Pallas kernels: 4.06 us -> 2.26 us  [shards(): pl.pallas_call(functools.partial(force_kernel, rows, copies, place), out_...]
    all_to_all x2, waiting for transfers between devices: 1.02 us -> 0.38 us  [from_slab(): lax.all_to_all(blocks, 'dom', 0, 0, axis_index_groups=[order], tiled=True)]
where the time goes in v8:
time: 33.1 us; the launch traced here: 33 us
  starting transfers between devices  18.5 us (56%)
  Pallas kernels  11.9 us (36%)
  between operations  1.97 us (6%)
  waiting for transfers between devices  0.55 us (2%)
    all_to_all x2, starting transfers between devices, from_slab(): lax.all_to_all(blocks, 'dom', 0, 0, axis_index_groups=[order], tiled=True)  17.9 us
    pallas_call x1, Pallas kernels, shards(): pl.pallas_call(functools.partial(solve_kernel, rows, domains, strides), o...  4.02 us
    pallas_call x1, Pallas kernels, shards(): pl.pallas_call(functools.partial(bond_kernel, rows, domains, strides), ou...  2.65 us
    pallas_call x1, Pallas kernels, shards(): pl.pallas_call(functools.partial(force_kernel, rows, copies, place), out_...  2.26 us
    pallas_call x1, Pallas kernels, shards(): pl.pallas_call(functools.partial(own_kernel, rows), out_shape=(jax.ShapeD...  1.54 us
    pallas_call x1, Pallas kernels, shards(): pl.pallas_call(functools.partial(pack_kernel, rows, copies), out_shape=(j...  1.44 us
  transfers between devices with their start and end apart: 4, of which 2 were waited for; matrix products, arithmetic and copies ran while one was open for 0% of the time, Pallas kernels for 13%

profile of v8, /device:TPU:0, one launch (start us, length us, event | category | flops | bytes accessed | tf_op | source)
XLA Modules:
  0.0 33.0 jit_solution(1831994920279410651)
XLA Ops:
  0.6 1.4 %pack.1 = (f32[192,128]{1,0:T(8,128)}, f32[8,128]{1,0:T(8,128)S(1)}) custom-call(f32[3,1,1,512]{3,2,1,0:T(1,128)} %coords_hbm.1, f32[1,1,512]{2,1,0:T(1,128)} %charge_hbm.1, f32[1,1,512]{2,1,0:T(1,128)} %mass_hbm.1, s32[2,1,1,256]{3,2,1,0:T(1,128)} %refs_3_.1, s32[2,1,1,128]{3,2,1,0:T(1,128)} %refs_4_.1), custom_call_target="tpu_custom_call" | custom-call | tf_op jit(solution)/shard_map/pack/pallas_call | solution.py:598
  2.1 9.3 %all-to-all-start = ((f32[8,24,128]{2,1,0:T(8,128)}), f32[8,24,128]{2,1,0:T(8,128)S(1)}, u32[]{:S(2)}, u32[]{:S(2)}) async-start(f32[8,24,128]{2,1,0:T(8,128)} %bitcast), calls=%async_computation | async-start | bytes 196608 | tf_op jit(solution)/shard_map/all_to_all | solution.py:33
  11.4 0.7 %collective-permute-start.1 = (f32[8,128]{1,0:T(8,128)S(1)}, f32[8,128]{1,0:T(8,128)S(1)}, u32[]{:S(2)}, u32[]{:S(2)}) collective-permute-start(f32[8,128]{1,0:T(8,128)S(1)} %get-tuple-element.11), channel_id=1, source_target_pairs={{0,24},{8,0},{16,8},{24,16},{1,25},{9,1},{17,9},{25,17},{2,26},{10... | collective-permute-start | bytes 12296 | tf_op jit(solution)/shard_map/ppermute | solution.py:23
  12.0 0.0 collective-permute-start
  13.3 1.5 %own.1 = (f32[4,512,128]{2,1,0:T(8,128)S(1)}, f32[4,64,128]{2,1,0:T(8,128)S(1)}, s32[64,128]{1,0:T(8,128)S(1)}, f32[17,128]{1,0:T(8,128)S(1)}) custom-call(f32[3,1,1,512]{3,2,1,0:T(1,128)} %coords_hbm.1, f32[1,1,512]{2,1,0:T(1,128)} %charge_hbm.1, f32[3,1,1,512]{3,2,1,0:T(1,128)} %velocity_hbm.1, f32[1,1,512]{2,1,0:T(1,128)} %mass_hbm.1, ...), custom_call_target="tpu_custom_call" | custom-call | flops 4194304 | bytes 1048576 | tf_op jit(solution)/shard_map/own/pallas_call | solution.py:613
  14.9 0.0 collective-permute-done.1.above_ref
  14.9 0.2 collective-permute-done.below_ref
  15.0 0.0 all-to-all-done
  15.0 2.3 %force.1 = f32[128,128]{1,0:T(8,128)} custom-call(s32[1,1]{1,0:T(1,128)S(6)} %copy.13.live_ref, s32[1,1]{1,0:T(1,128)S(6)} %copy.14.count_ref, s32[1,1,64]{2,1,0:T(1,128)} %block_hbm.1, f32[192,128]{1,0:T(8,128)S(1)} %bitcast.4, f32[8,128]{1,0:T(8,128)S(1)} %collective-permute-done.below_ref, f32[8,128]{1,0:T(8,128)S(1)} %collective-permute-done.1.above_ref, ...), custom_call_target="tpu_custom_call" | custom-call | flops 31457280 | bytes 98304 | tf_op jit(solution)/shard_map/force/pallas_call | solution.py:644
  17.3 8.6 %all-to-all-start.1 = ((f32[8,16,128]{2,1,0:T(8,128)}), f32[8,16,128]{2,1,0:T(8,128)S(1)}, u32[]{:S(2)}, u32[]{:S(2)}) async-start(f32[8,16,128]{2,1,0:T(8,128)} %bitcast.2), calls=%async_computation.1 | async-start | bytes 131072 | tf_op jit(solution)/shard_map/all_to_all | solution.py:33
  25.9 2.7 %bonds.1 = (f32[144,128]{1,0:T(8,128)S(1)}, bf16[6144,256]{1,0:T(8,128)(2,1)S(1)}) custom-call(f32[192,128]{1,0:T(8,128)S(1)} %bitcast.5), custom_call_target="tpu_custom_call" | custom-call | flops 12582912 | bytes 98304 | tf_op jit(solution)/shard_map/bonds/pallas_call | solution.py:665
  28.6 0.4 %all-to-all-done.1 = f32[8,16,128]{2,1,0:T(8,128)S(1)} async-done(((f32[8,16,128]{2,1,0:T(8,128)}), f32[8,16,128]{2,1,0:T(8,128)S(1)}, u32[]{:S(2)}, u32[]{:S(2)}) %all-to-all-start.1) | async-done | bytes 65568 | tf_op jit(solution)/shard_map/all_to_all | solution.py:33
  28.9 4.0 %solve.1 = (f32[3,1,1,512]{3,2,1,0:T(1,128)}, f32[3,1,1,512]{3,2,1,0:T(1,128)}) custom-call(f32[192,128]{1,0:T(8,128)S(1)} %bitcast.6, f32[128,128]{1,0:T(8,128)S(1)} %bitcast.7, f32[144,128]{1,0:T(8,128)S(1)} %get-tuple-element.16.weight_ref, bf16[6144,256]{1,0:T(8,128)(2,1)S(1)} %get-tuple-element.17.matrix_ref), custom_call_target="tpu_custom_call" | custom-call | tf_op jit(solution)/shard_map/solve/pallas_call | solution.py:680
Async XLA Ops:
  2.1 13.0 %all-to-all-start = ((f32[8,24,128]{2,1,0:T(8,128)}), f32[8,24,128]{2,1,0:T(8,128)S(1)}, u32[]{:S(2)}, u32[]{:S(2)}) async-start(f32[8,24,128]{2,1,0:T(8,128)} %bitcast), calls=%async_computation | async-start | bytes 196608 | tf_op jit(solution)/shard_map/all_to_all | solution.py:33
  11.4 3.5 %collective-permute-start.1 = (f32[8,128]{1,0:T(8,128)S(1)}, f32[8,128]{1,0:T(8,128)S(1)}, u32[]{:S(2)}, u32[]{:S(2)}) collective-permute-start(f32[8,128]{1,0:T(8,128)S(1)} %get-tuple-element.11), channel_id=1, source_target_pairs={{0,24},{8,0},{16,8},{24,16},{1,25},{9,1},{17,9},{25,17},{2,26},{10... | collective-permute-start | bytes 12296 | tf_op jit(solution)/shard_map/ppermute | solution.py:23
  12.0 3.0 %collective-permute-start = (f32[8,128]{1,0:T(8,128)S(1)}, f32[8,128]{1,0:T(8,128)S(1)}, u32[]{:S(2)}, u32[]{:S(2)}) collective-permute-start(f32[8,128]{1,0:T(8,128)S(1)} %get-tuple-element.11), channel_id=1, source_target_pairs={{0,8},{8,16},{16,24},{24,0},{1,9},{9,17},{17,25},{25,1},{2,10},{10... | collective-permute-start | bytes 12296 | tf_op jit(solution)/shard_map/ppermute | solution.py:23
  17.3 11.6 %all-to-all-start.1 = ((f32[8,16,128]{2,1,0:T(8,128)}), f32[8,16,128]{2,1,0:T(8,128)S(1)}, u32[]{:S(2)}, u32[]{:S(2)}) async-start(f32[8,16,128]{2,1,0:T(8,128)} %bitcast.2), calls=%async_computation.1 | async-start | bytes 131072 | tf_op jit(solution)/shard_map/all_to_all | solution.py:33
